TPU v7x, 768 devices: a whole 4x8x12 slice. The times are simulated.
768 devices in a mesh: seq: 16 (over y, core), fsdp: 48 (over z, x).
Axes of the slice: x: 4, y: 8, z: 12, core: 2. Of those that a mesh axis runs over, the one named last changes fastest.
Arguments:
- sel_inputs: bfloat16 [48, 1024, 4096], P('fsdp', 'seq'), may hold values from -6 to 6
- val_grads: bfloat16 [48, 1024, 1024], P('fsdp', 'seq'), may hold values from -6 to 6
- positions: int32 [48, 512], P('fsdp'), may hold values from 0 to 4095, as said below
- value_weight: bfloat16 [4096, 1024], P('seq'), may hold values from -0.1875 to 0.1875
- norm_gain: float32 [4096], P('seq'), may hold values from 0.25 to 1.75
Outputs:
- input_grad: bfloat16 [48, 1024, 4096], P('fsdp', 'seq')
- weight_grad: float32 [4096, 1024], P('seq')
- gain_grad: float32 [4096], P('seq')
Inputs may be any that keep to these rules, and one draw needn't show every extreme that they name: Each sequence's positions are distinct and increasing; the number that falls in each device's 256 positions is a multiple of 4 and at most 64, and some device of every sequence holds exactly 64.
All inputs are finite; a program needn't handle non-finite values.
Results may differ from a plain program's by a relative error of at most 0.003.
Values may be sent and summed in bfloat16 or wider, within the bound.
No kernel may reach another device: no remote copies, remote signals or barrier semaphores. Data moves between devices by JAX's collectives and lax.ppermute only.
A program may use at most 32 MiB of HBM per device.

v0:
```python
import jax
import jax.numpy as jnp
from jax import lax
from jax.sharding import PartitionSpec as P

D = 4096
TOK_DEV = 256


EPS = 1e-05


def column_work(rows_x, rows_dv, live, norm_gain, value_weight):
    columns = lax.all_to_all(rows_x, "seq", split_axis=1, concat_axis=0, tiled=True)
    dv_all = lax.all_gather(rows_dv, "seq", axis=0, tiled=True)
    values = columns.astype(jnp.float32)
    dnormed = lax.dot_general(
        dv_all, value_weight, (((1,), (1,)), ((), ())), preferred_element_type=jnp.float32
    )
    gained = dnormed * norm_gain[None, :]
    squares = lax.psum(jnp.sum(values * values, axis=1), "seq")
    inv = lax.rsqrt(squares / D + EPS) * live
    normed = values * inv[:, None]
    row_total = lax.psum(jnp.sum(gained * normed, axis=1), "seq")
    mean_term = row_total / D
    scaled = (normed * norm_gain[None, :]).astype(jnp.bfloat16)
    result_cols = (inv[:, None] * (gained - normed * mean_term[:, None])).astype(jnp.bfloat16)
    grad_w = lax.dot_general(
        scaled, dv_all, (((0,), (0,)), ((), ())), preferred_element_type=jnp.float32
    )
    grad_g = jnp.sum(dnormed * normed, axis=0)
    result_rows = lax.all_to_all(result_cols, "seq", split_axis=0, concat_axis=1, tiled=True)
    return (result_rows, grad_w, grad_g)


def body(sel_inputs, val_grads, positions, value_weight, norm_gain):
    inputs = sel_inputs[0]
    grads = val_grads[0]
    places = positions[0]
    nseq = lax.axis_size("seq")
    rows = inputs.shape[0]
    devices = jnp.arange(nseq, dtype=jnp.int32)
    counts = jnp.sum(((places // TOK_DEV)[:, None] == devices[None, :]).astype(jnp.int32), axis=0)
    slot_ids = jnp.arange(nseq * rows, dtype=jnp.int32)
    live = (slot_ids % rows < counts[slot_ids // rows]).astype(jnp.float32)
    result, grad_w, grad_g = column_work(inputs, grads, live, norm_gain, value_weight)
    grad_w, grad_g = lax.psum((grad_w, grad_g), "fsdp")
    return (result[None], grad_w, grad_g)


def solution(mesh):
    placed = (
        P("fsdp", "seq", None),
        P("fsdp", "seq", None),
        P("fsdp", None),
        P("seq", None),
        P("seq"),
    )
    return jax.shard_map(
        body,
        mesh=mesh,
        in_specs=placed,
        out_specs=(P("fsdp", "seq", None), P("seq", None), P("seq")),
        check_vma=False,
    )
```

profile of v0, /device:TPU:8, one launch (start us, length us, event | category | flops | bytes accessed | tf_op | source)
XLA Modules:
  0.0 335.0 jit_solution(12167091226798674959)
XLA Ops:
  7.2 0.0 all-gather.3.cloned.1.call-start
  7.2 0.7 all-gather.3.cloned.1.call-update
  7.9 1.1 copy.14
  9.1 1.0 copy.12
  10.0 12.8 %all-to-all-start = ((bf16[64,16,256]{2,0,1:T(8,128)(2,1)}), bf16[64,16,256]{2,0,1:T(8,128)(2,1)S(1)}, u32[]{:S(2)}, u32[]{:S(2)}) async-start(bf16[64,16,256]{2,0,1:T(8,128)(2,1)} %copy.12), calls=%async_computation | async-start | bytes 1048576 | tf_op jit(solution)/shard_map/all_to_all | solution.py:14
  22.9 0.0 all-reduce.2.cloned.1.call-start
  23.2 0.1 convert_reduce_fusion
  23.4 0.7 fusion.10
  24.1 4.5 %compare_select_fusion.1 = s32[1024,1]{0,1:T(1,128)S(1)} fusion(s32[]{:T(128)} %bitcast.10, s32[]{:T(128)} %bitcast.11, s32[]{:T(128)} %bitcast.12, s32[]{:T(128)} %bitcast.13, s32[]{:T(128)} %bitcast.14, s32[]{:T(128)} %bitcast.16, s32[]{:T(128)} %bitcast.15), kind=kLoop, calls=%fused_computation.22 | loop fusion | flops 23552 | bytes 4124 | tf_op jit(solution)/shard_map/gather | solution.py:45
  28.5 8.7 %all-to-all-done = bf16[64,16,256]{2,0,1:T(8,128)(2,1)S(1)} async-done(((bf16[64,16,256]{2,0,1:T(8,128)(2,1)}), bf16[64,16,256]{2,0,1:T(8,128)(2,1)S(1)}, u32[]{:S(2)}, u32[]{:S(2)}) %all-to-all-start) | async-done | bytes 524320 | tf_op jit(solution)/shard_map/all_to_all | solution.py:14
  37.2 0.2 multiply_reduce_fusion.2
  37.4 0.1 reduce_sum.43
  37.5 24.0 %psum.28 = f32[1024]{0:T(1024)S(1)} all-reduce(f32[1024]{0:T(1024)S(1)} %reduce_sum.43), channel_id=1, replica_groups=mesh['seq'=16,'fsdp'=48] {'seq'}, use_global_device_ids=true, to_apply=%region_2.3 | all-reduce | flops 1024 | bytes 8192 | tf_op jit(solution)/shard_map/psum | solution.py:21
  61.5 5.5 %rsqrt_select_fusion = f32[1024]{0:T(1024)S(1)} fusion(f32[1024]{0:T(1024)S(1)} %psum.28, pred[1024]{0:T(1024)(128)(4,1)S(1)} %compare_reduce_fusion, pred[1024]{0:T(1024)(128)(4,1)S(1)} %compare_reduce_fusion.1, pred[1024]{0:T(1024)(128)(4,1)S(1)} %compare_reduce_fusion.2, pred[1024]{0:T(1024)(128)(4,1)S(1)} %compare_reduce_fusion.3, ...), kind=kLoop, calls=%fused_computation.34 | loop fusion | flops 19456 | bytes 21540 | tf_op jit(solution)/shard_map/mul | solution.py:22
  67.1 3.6 %multiply_reduce_fusion = (f32[256]{0:T(256)S(1)}, f32[1024]{0:T(1024)S(1)}, bf16[1024,256]{1,0:T(8,128)(2,1)}, f32[1024,256]{1,0:T(8,128)}) fusion(bf16[64,16,256]{2,0,1:T(8,128)(2,1)S(1)} %all-to-all-done, f32[1024]{0:T(1024)S(1)} %rsqrt_select_fusion, f32[256]{0:T(256)S(1)} %copy-done.3, bf16[256,1024]{1,0:T(8,128)(2,1)S(1)} %copy-done, ...), kind=kOutput, calls=%fused_computation.5 | convolution fusion | flops 539228928 | bytes 4728832 | tf_op jit(solution)/shard_map/dot_general | solution.py:17
  70.7 23.5 %psum.29 = f32[1024]{0:T(1024)S(1)} all-reduce(f32[1024]{0:T(1024)S(1)} %get-tuple-element.4), channel_id=1, replica_groups=mesh['seq'=16,'fsdp'=48] {'seq'}, use_global_device_ids=true, to_apply=%region_4.5 | all-reduce | flops 1024 | bytes 8192 | tf_op jit(solution)/shard_map/psum | solution.py:24
  94.3 2.8 fusion
  97.1 2.4 multiply_convert_fusion.1
  99.5 9.1 %all-to-all-start.1 = ((bf16[16,64,256]{2,1,0:T(8,128)(2,1)}), bf16[16,64,256]{2,1,0:T(8,128)(2,1)S(1)}, u32[]{:S(2)}, u32[]{:S(2)}) async-start(bf16[16,64,256]{2,1,0:T(8,128)(2,1)} %bitcast.22), calls=%async_computation.1 | async-start | bytes 1048576 | tf_op jit(solution)/shard_map/all_to_all | solution.py:32
  108.6 115.2 %psum.31 = f32[256]{0:T(256)} all-reduce(f32[256]{0:T(256)S(1)} %get-tuple-element.3), channel_id=1, replica_groups=mesh['seq'=16,'fsdp'=48] {'fsdp'}, use_global_device_ids=true, to_apply=%region_7.8 | all-reduce | flops 256 | bytes 2048 | tf_op jit(solution)/shard_map/psum | solution.py:47
  223.8 0.3 copy.13
  224.1 1.0 broadcast_in_dim.2
  225.1 100.7 %all-reduce.2.cloned.1.call-done = f32[256,1024]{1,0:T(8,128)} async-done(((f32[256,1024]{1,0:T(8,128)}), f32[256,1024]{1,0:T(8,128)}) %all-reduce.2.cloned.1.call-update) | async-done | bytes 1048592 | tf_op jit(solution)/shard_map/psum | solution.py:47
  325.8 2.3 copy.16
  (22 shorter events, 0.4 us)
Async XLA Ops:
  7.2 59.9 %copy-start = (bf16[256,1024]{1,0:T(8,128)(2,1)S(1)}, bf16[256,1024]{1,0:T(8,128)(2,1)}, u32[]{:S(2)}) copy-start(bf16[256,1024]{1,0:T(8,128)(2,1)} %param.8) | copy-start | bytes 1572868
  7.2 16.1 %copy-start.2 = (s32[1,512]{1,0:T(1,128)S(1)}, s32[1,512]{1,0:T(1,128)}, u32[]{:S(2)}) copy-start(s32[1,512]{1,0:T(1,128)} %param.7) | copy-start | bytes 6148
  7.2 59.9 %copy-start.3 = (f32[256]{0:T(256)S(1)}, f32[256]{0:T(256)}, u32[]{:S(2)}) copy-start(f32[256]{0:T(256)} %param.9) | copy-start | bytes 3076
  7.2 59.9 %all-gather.3.cloned.1.call-start = ((), (), s32[]{:S(2)}) async-start(), calls=%async_computation.3 | async-start | bytes 2228224 | tf_op jit(solution)/shard_map/all_gather | solution.py:15
  10.0 27.2 %all-to-all-start = ((bf16[64,16,256]{2,0,1:T(8,128)(2,1)}), bf16[64,16,256]{2,0,1:T(8,128)(2,1)S(1)}, u32[]{:S(2)}, u32[]{:S(2)}) async-start(bf16[64,16,256]{2,0,1:T(8,128)(2,1)} %copy.12), calls=%async_computation | async-start | bytes 1048576 | tf_op jit(solution)/shard_map/all_to_all | solution.py:14
  22.9 302.9 %all-reduce.2.cloned.1.call-start = ((), (), s32[]{:S(2)}) async-start(), calls=%async_computation.2 | async-start | bytes 2097152 | tf_op jit(solution)/shard_map/psum | solution.py:47
  67.1 27.2 %copy-start.1 = (bf16[1,1024,1024]{2,1,0:T(8,128)(2,1)S(1)}, bf16[1,1024,1024]{2,1,0:T(8,128)(2,1)}, u32[]{:S(2)}) copy-start(bf16[1,1024,1024]{2,1,0:T(8,128)(2,1)} %all-gather.3.cloned.1.call-done) | copy-start | bytes 6291460
  99.5 124.3 %all-to-all-start.1 = ((bf16[16,64,256]{2,1,0:T(8,128)(2,1)}), bf16[16,64,256]{2,1,0:T(8,128)(2,1)S(1)}, u32[]{:S(2)}, u32[]{:S(2)}) async-start(bf16[16,64,256]{2,1,0:T(8,128)(2,1)} %bitcast.22), calls=%async_computation.1 | async-start | bytes 1048576 | tf_op jit(solution)/shard_map/all_to_all | solution.py:32
Sparse Core Ops, SparseCore 0:
  10.4 51.6 all-gather.2
  97.2 228.5 all-reduce.1
where the time goes:
time: 336 us; the launch traced here: 335 us
  blocking collectives  163 us (49%)
  waiting for transfers between devices  110 us (33%)
  starting transfers between devices  22 us (7%)
  between operations  14.1 us (4%)
  other arithmetic  13 us (4%)
  local copies, waits for them, and re-layouts  6.53 us (2%)
  matrix products  6.41 us (2%)
    psum x1, blocking collectives, body(): grad_w, grad_g = lax.psum((grad_w, grad_g), 'fsdp')  115 us
    psum x1, waiting for transfers between devices, body(): grad_w, grad_g = lax.psum((grad_w, grad_g), 'fsdp')  101 us
    psum x1, blocking collectives, column_work(): squares = lax.psum(jnp.sum(values * values, axis=1), 'seq')  24 us
    psum x1, blocking collectives, column_work(): row_total = lax.psum(jnp.sum(gained * normed, axis=1), 'seq')  23.5 us
    all_to_all x1, starting transfers between devices, column_work(): lax.all_to_all(rows_x, 'seq', split_axis=1, concat_axis=0, tiled=True)  12.8 us
    all_to_all x1, starting transfers between devices, column_work(): lax.all_to_all(result_cols, 'seq', split_axis=0, concat_axis=1, tiled=True)  9.1 us
    all_to_all x1, waiting for transfers between devices, column_work(): lax.all_to_all(rows_x, 'seq', split_axis=1, concat_axis=0, tiled=True)  8.67 us
  transfers between devices with their start and end apart: 4, of which 2 were waited for; matrix products, arithmetic and copies ran while one was open for 5% of the time, Pallas kernels for 0%

commit v1 on v0

v1 whole, which is shorter than its diff:
```python
import jax
import jax.numpy as jnp
from jax import lax
from jax.experimental import pallas as pl
from jax.experimental.pallas import tpu as pltpu
from jax.sharding import Mesh
from jax.sharding import PartitionSpec as P

D = 4096
KVW = 1024
TOK_DEV = 256
ROWS = 64
EPS = 1e-05
LANES = 128
CHIPS = 8
OWN = D // CHIPS // 2
PLANE = ("zl", "x")
DEEP = "zh"
SWAP = ((0, 1), (1, 0))
F32 = jnp.float32
BF16 = jnp.bfloat16
VMEM = pl.BlockSpec(memory_space=pltpu.VMEM)
SMEM = pl.BlockSpec(memory_space=pltpu.SMEM)


def call(kernel, n_scalars, outs, *args, flops=0, limit=24):
    shapes = [jax.ShapeDtypeStruct(shape, dtype) for shape, dtype in outs]
    sizes = [a.size * a.dtype.itemsize for a in (*args, *shapes)]
    return pl.pallas_call(
        kernel,
        out_shape=shapes,
        in_specs=[SMEM] * n_scalars + [VMEM] * (len(args) - n_scalars),
        out_specs=[VMEM] * len(shapes),
        compiler_params=pltpu.CompilerParams(vmem_limit_bytes=limit << 20),
        cost_estimate=pl.CostEstimate(flops=flops, bytes_accessed=sum(sizes), transcendentals=0),
    )(*args)


def rounded(value):
    return value.astype(BF16).astype(F32)


def exchange(blocks, axis):
    return lax.all_to_all(blocks, axis, 0, 0, tiled=True)


def spread(block, axis):
    return exchange(jnp.broadcast_to(block[None], (lax.axis_size(axis),) + block.shape), axis)


def prepare_kernel(first_ref, places_ref, x_ref, dv_ref, slices_ref, inv_ref):
    first = first_ref[0]
    places = places_ref[...]
    inside = jnp.where((places >= first) & (places < first + TOK_DEV), 1.0, 0.0)
    count = jnp.sum(inside, axis=1, keepdims=True)
    width = D // CHIPS
    squares = jnp.zeros((ROWS, LANES), F32)
    for j in range(CHIPS):
        block = x_ref[:, j * width:(j + 1) * width]
        slices_ref[j, :, :width] = block
        for k in range(0, width, LANES):
            part = block[:, k:k + LANES].astype(F32)
            squares = squares + part * part
    squares = jnp.sum(squares, axis=1, keepdims=True)
    row = lax.broadcasted_iota(jnp.int32, (ROWS, 1), 0).astype(F32)
    inv = jnp.where(row < count, lax.rsqrt(squares / D + EPS), 0.0)
    inv_ref[...] = jnp.broadcast_to(inv, (ROWS, LANES))
    high = rounded(inv)
    middle = rounded(inv - high)
    low = (inv - high) - middle
    lane = lax.broadcasted_iota(jnp.int32, (ROWS, LANES), 1)
    last = dv_ref[:, KVW - 1:].astype(F32)
    extra = jnp.where(lane == 0, last, jnp.where(lane == 1, high, jnp.where(lane == 2, middle, jnp.where(lane == 3, low, 0.0))))
    extra = extra.astype(BF16)
    for j in range(CHIPS):
        slices_ref[j, :, width:] = extra


def products_kernel(core_ref, columns_ref, dv_ref, mine_w, other_w, mine_g, other_g, back_ref, keep_ref, send_ref):
    core = core_ref[0]
    width = D // CHIPS
    extra = columns_ref[:, :, width:].reshape(CHIPS * ROWS, LANES).astype(F32)
    inv = extra[:, 1:2] + extra[:, 2:3] + extra[:, 3:4]
    dv = dv_ref[...]
    for half, w_ref, g_ref, out_ref in ((1 - core, other_w, other_g, send_ref), (core, mine_w, mine_g, keep_ref)):
        at = pl.multiple_of(half * OWN, OWN)
        dnormed = lax.dot_general(dv, w_ref[...], (((1,), (1,)), ((), ())), preferred_element_type=F32)
        gain = g_ref[...]
        back_ref[:, :, pl.ds(at, OWN)] = (dnormed * gain).reshape(CHIPS, ROWS, OWN)
        normed = columns_ref[:, :, pl.ds(at, OWN)].reshape(CHIPS * ROWS, OWN).astype(F32) * inv
        scaled = (normed * gain).astype(BF16)
        out_ref[:OWN, :] = lax.dot_general(scaled, dv, (((0,), (0,)), ((), ())), preferred_element_type=F32)
        out_ref[OWN:, :] = jnp.zeros((8, KVW), F32)
        out_ref[OWN:OWN + 1, :OWN] = jnp.sum(dnormed * normed, axis=0, keepdims=True)


def blocks_kernel(keep_ref, theirs_ref, blocks_ref):
    gain = keep_ref[OWN:OWN + 1, :OWN] + theirs_ref[OWN:OWN + 1, :OWN]
    row = lax.broadcasted_iota(jnp.int32, (16, LANES), 0)
    high = rounded(gain)
    rest = gain - high
    extra = jnp.zeros((16, LANES), F32)
    for i, part in enumerate((high[:, :LANES], high[:, LANES:], rest[:, :LANES], rest[:, LANES:])):
        extra = jnp.where(row == i, part, extra)
    extra = extra.astype(BF16)
    for j in range(16):
        rows = slice(j * 16, (j + 1) * 16)
        blocks_ref[j, :, :KVW] = (keep_ref[rows, :] + theirs_ref[rows, :]).astype(BF16)
        blocks_ref[j, :, KVW:] = extra


def finish_kernel(whole_ref, w_ref, g_ref):
    for j in range(16):
        w_ref[j * 16:(j + 1) * 16, :] = whole_ref[j, :, :KVW].astype(F32)
    extra = whole_ref[0, :, KVW:].astype(F32)
    g_ref[...] = extra[0:2] + extra[2:4]


def rows_kernel(me_ref, x_ref, inv_ref, *refs):
    blocks, out_ref = refs[:-1], refs[-1]
    width = D // CHIPS
    me = me_ref[0]
    spots = [pl.multiple_of(lax.rem(me + CHIPS - k, CHIPS) * width, width) for k in range(CHIPS)]
    total = jnp.zeros((ROWS, LANES), F32)
    for at, block in zip(spots, blocks):
        product = block[...] * x_ref[:, pl.ds(at, width)].astype(F32)
        for k in range(0, width, LANES):
            total = total + product[:, k:k + LANES]
    inv = inv_ref[:, :1]
    mean = inv * (jnp.sum(total, axis=1, keepdims=True) / D)
    shift = inv * mean
    for at, block in zip(spots, blocks):
        values = x_ref[:, pl.ds(at, width)].astype(F32)
        out_ref[:, pl.ds(at, width)] = (inv * (block[...] - values * shift)).astype(BF16)


def sum_gain(part):
    row = lax.broadcasted_iota(jnp.int32, part.shape, 0)
    lane = lax.broadcasted_iota(jnp.int32, part.shape, 1)
    both = part + jnp.concatenate([part[2:], part[:2]])
    return jnp.where((lane >= KVW) & (row < 2), both, part)


def split_gain(part):
    row = lax.broadcasted_iota(jnp.int32, part.shape, 0)
    lane = lax.broadcasted_iota(jnp.int32, part.shape, 1)
    rest = part - lax.reduce_precision(part, 8, 7)
    rest = jnp.concatenate([rest[-2:], rest[:-2]])
    part = jnp.where((lane >= KVW) & (row >= 2) & (row < 4), rest, part)
    return part.astype(BF16)


def body(sel_inputs, val_grads, positions, value_weight, norm_gain):
    inputs, grads = sel_inputs[0], val_grads[0]
    chip, core = lax.axis_index("y"), lax.axis_index("core")
    first = ((chip * 2 + core) * TOK_DEV).reshape(1)
    width = D // CHIPS
    slices, inv = call(
        prepare_kernel, 1,
        [((CHIPS, ROWS, width + LANES), BF16), ((ROWS, LANES), F32)],
        first, positions, inputs, grads,
    )
    columns = exchange(slices, "y")
    other_weight = lax.ppermute(value_weight, "core", SWAP)
    gain = norm_gain.reshape(1, OWN)
    other_gain = lax.ppermute(gain, "core", SWAP)
    most = lax.all_gather(grads[:, :KVW - 1], "y", axis=0, tiled=True)
    last = columns[:, :, width:width + 1].reshape(CHIPS * ROWS, 1)
    grads_all = jnp.concatenate([most, last], axis=1)

    back, keep, send = call(
        products_kernel, 1,
        [((CHIPS, ROWS, width), F32), ((OWN + 8, KVW), F32), ((OWN + 8, KVW), F32)],
        core.reshape(1), columns, grads_all, value_weight, other_weight, gain, other_gain,
        flops=4 * CHIPS * ROWS * width * KVW,
    )
    theirs = lax.ppermute(send, "core", SWAP)
    (blocks,) = call(blocks_kernel, 0, [((16, 16, KVW + LANES), BF16)], keep, theirs)
    part = sum_gain(jnp.sum(exchange(blocks, PLANE).astype(F32), axis=0))

    def moved(k):
        block = lax.dynamic_index_in_dim(back, (chip + k) % CHIPS, 0, keepdims=False)
        if k == 0:
            return block
        return lax.ppermute(block, "y", [(i, (i + k) % CHIPS) for i in range(CHIPS)])

    rows = {k: moved(k) for k in EARLY}
    if EARLY:
        part, rows = lax.optimization_barrier((part, rows))
    one = lax.ppermute(part, DEEP, [(i, (i + 1) % 3) for i in range(3)])
    two = lax.ppermute(part, DEEP, [(i, (i + 2) % 3) for i in range(3)])
    at = lax.axis_index(DEEP)
    zeroth = jnp.where(at == 0, part, jnp.where(at == 1, one, two))
    second = jnp.where(at == 2, part, jnp.where(at == 0, one, two))
    middle = jnp.where(at == 1, part, jnp.where(at == 2, one, two))
    part = split_gain((zeroth + middle) + second)
    whole = spread(part, PLANE)
    rows.update({k: moved(k) for k in range(CHIPS) if k not in EARLY})

    (result,) = call(
        rows_kernel, 1, [((ROWS, D), BF16)],
        chip.reshape(1), inputs, inv, *[rows[k] for k in range(CHIPS)],
    )
    weight_grad, gain_grad = call(
        finish_kernel, 0, [((OWN, KVW), F32), ((2, LANES), F32)], whole
    )
    return result[None], weight_grad, gain_grad.reshape(OWN)


EARLY = (4, 3, 5, 2)


def solution(mesh):
    fine = Mesh(
        mesh.devices.reshape(8, 2, 3, 4, 4), ("y", "core", "zh", "zl", "x")
    )
    seq, fsdp = ("y", "core"), ("zh", "zl", "x")
    return jax.shard_map(
        body,
        mesh=fine,
        in_specs=(P(fsdp, seq, None), P(fsdp, seq, None), P(fsdp, None), P(seq, None), P(seq)),
        out_specs=(P(fsdp, seq, None), P(seq, None), P(seq)),
        check_vma=False,
    )
```

time: 336 us -> 151 us (0.45)
  the two profiles are of different devices: /device:TPU:8 before, /device:TPU:2 now
where the time goes in v1:
time: 151 us; the launch traced here: 150 us
  starting transfers between devices  73.2 us (48%)
  blocking collectives  37.1 us (25%)
  waiting for transfers between devices  27.3 us (18%)
  Pallas kernels  5.8 us (4%)
  local copies, waits for them, and re-layouts  3.67 us (2%)
  other arithmetic  1.68 us (1%)
    all_gather x1, blocking collectives, body(): most = lax.all_gather(grads[:, :KVW - 1], 'y', axis=0, tiled=True)  37.1 us
    ppermute x7, starting transfers between devices, moved(): lax.ppermute(block, 'y', [(i, (i + k) % CHIPS) for i in range(CHIPS)])  28.3 us
    all_to_all x3, starting transfers between devices, exchange(): return lax.all_to_all(blocks, axis, 0, 0, tiled=True)  24.9 us
    ppermute x7, waiting for transfers between devices, moved(): lax.ppermute(block, 'y', [(i, (i + k) % CHIPS) for i in range(CHIPS)])  15.7 us
    ppermute x1, starting transfers between devices, body(): one = lax.ppermute(part, DEEP, [(i, (i + 1) % 3) for i in range(3)])  10.6 us
    ppermute x1, waiting for transfers between devices, body(): two = lax.ppermute(part, DEEP, [(i, (i + 2) % 3) for i in range(3)])  8.37 us
    pallas_call x5, Pallas kernels, call(): pl.pallas_call(kernel, out_shape=shapes, in_specs=[SMEM] * n_scalars + [V...  5.8 us
    ppermute x1, starting transfers between devices, body(): two = lax.ppermute(part, DEEP, [(i, (i + 2) % 3) for i in range(3)])  3.15 us
  transfers between devices with their start and end apart: 15, of which 7 were waited for; matrix products, arithmetic and copies ran while one was open for 1% of the time, Pallas kernels for 1%

profile of v1, /device:TPU:2, one launch (start us, length us, event | category | flops | bytes accessed | tf_op | source)
XLA Modules:
  0.0 149.7 jit_solution(137177232134006634)
XLA Ops:
  4.4 7.1 %all-to-all-start = ((bf16[8,64,640]{2,1,0:T(8,128)(2,1)}), bf16[8,64,640]{2,1,0:T(8,128)(2,1)S(1)}, u32[]{:S(2)}, u32[]{:S(2)}) async-start(bf16[8,64,640]{2,1,0:T(8,128)(2,1)} %get-tuple-element.16), calls=%async_computation | async-start | bytes 1310720 | tf_op jit(solution)/shard_map/all_to_all | solution.py:44
  11.5 1.9 %collective-permute-start = (bf16[256,1024]{1,0:T(8,128)(2,1)S(1)}, bf16[256,1024]{1,0:T(8,128)(2,1)S(1)}, u32[]{:S(2)}, u32[]{:S(2)}) collective-permute-start(bf16[256,1024]{1,0:T(8,128)(2,1)S(1)} %copy-done.5), channel_id=1, source_target_pairs={{0,48},{48,0},{1,49},{49,1},{2,50},{50,2},{3,51},{51,3},{4,52},{52... | collective-permute-start | bytes 1572872 | tf_op jit(solution)/shard_map/ppermute | solution.py:164
  13.4 2.4 %collective-permute-start.1 = (f32[1,256]{1,0:T(1,128)S(1)}, f32[1,256]{1,0:T(1,128)S(1)}, u32[]{:S(2)}, u32[]{:S(2)}) collective-permute-start(f32[1,256]{1,0:T(1,128)S(1)} %bitcast.31), channel_id=1, source_target_pairs={{0,48},{48,0},{1,49},{49,1},{2,50},{50,2},{3,51},{51,3},{4,52},{52... | collective-permute-start | bytes 3080 | tf_op jit(solution)/shard_map/ppermute | solution.py:166
  15.9 37.1 %all_gather.3 = bf16[512,1023]{1,0:T(8,128)(2,1)} all-gather(bf16[64,1023]{1,0:T(8,128)(2,1)S(1)} %bitcast.30), channel_id=1, replica_groups=mesh['y'=8,'core'=2,'zh'=3,'zl'=4,'x'=4] {'y'}, dimensions={0}, use_global_device_ids=true | all-gather | bytes 1178496 | tf_op jit(solution)/shard_map/all_gather | solution.py:167
  53.0 1.4 pad_maximum_fusion.dv_ref
  54.4 1.6 %shard_map.77 = (f32[8,64,512]{2,1,0:T(8,128)S(1)}, f32[264,1024]{1,0:T(8,128)S(1)}, f32[264,1024]{1,0:T(8,128)S(1)}) custom-call(s32[1]{0:T(128)} %bitcast.4.core_ref, bf16[8,64,640]{2,1,0:T(8,128)(2,1)S(1)} %all-to-all-done.columns_ref, bf16[512,1024]{1,0:T(8,128)(2,1)S(1)} %pad_maximum_fusion.dv_ref, bf16[256,1024]{1,0:T(8,128)(2,1)S(1)} %copy-done.5, ...), custom_call_target="tpu_custom_call" | custom-call | flops 1073741824 | bytes 5965828 | tf_op jit(solution)/shard_map/pallas_call | solution.py:29
  55.9 1.9 %collective-permute-start.3 = (f32[264,1024]{1,0:T(8,128)S(1)}, f32[264,1024]{1,0:T(8,128)S(1)}, u32[]{:S(2)}, u32[]{:S(2)}) collective-permute-start(f32[264,1024]{1,0:T(8,128)S(1)} %get-tuple-element.19), channel_id=1, source_target_pairs={{0,48},{48,0},{1,49},{49,1},{2,50},{50,2},{3,51},{51,3},{4,52},{52... | collective-permute-start | bytes 3244040 | tf_op jit(solution)/shard_map/ppermute | solution.py:177
  57.9 2.7 %collective-permute-done.3.theirs_ref = f32[264,1024]{1,0:T(8,128)S(1)} collective-permute-done((f32[264,1024]{1,0:T(8,128)S(1)}, f32[264,1024]{1,0:T(8,128)S(1)}, u32[]{:S(2)}, u32[]{:S(2)}) %collective-permute-start.3) | collective-permute-done | bytes 1081376 | tf_op jit(solution)/shard_map/ppermute | solution.py:177
  61.5 10.3 %all-to-all-start.1 = ((bf16[16,16,1152]{2,1,0:T(8,128)(2,1)}), bf16[16,16,1152]{2,1,0:T(8,128)(2,1)S(1)}, u32[]{:S(2)}, u32[]{:S(2)}) async-start(bf16[16,16,1152]{2,1,0:T(8,128)(2,1)} %shard_map.78), calls=%async_computation.1 | async-start | bytes 1179648 | tf_op jit(solution)/shard_map/all_to_all | solution.py:44
  71.9 3.3 %collective-permute-start.4 = (f32[64,512]{1,0:T(8,128)S(1)}, f32[64,512]{1,0:T(8,128)S(1)}, u32[]{:S(2)}, u32[]{:S(2)}) collective-permute-start(f32[64,512]{1,0:T(8,128)S(1)} %get-tuple-element.34), channel_id=1, source_target_pairs={{0,192},{96,288},{192,384},{288,480},{384,576},{480,672},{576,0},{... | collective-permute-start | bytes 393224 | tf_op jit(solution)/shard_map/ppermute | solution.py:185
  75.2 5.4 %collective-permute-start.5 = (f32[64,512]{1,0:T(8,128)S(1)}, f32[64,512]{1,0:T(8,128)S(1)}, u32[]{:S(2)}, u32[]{:S(2)}) collective-permute-start(f32[64,512]{1,0:T(8,128)S(1)} %get-tuple-element.33), channel_id=1, source_target_pairs={{0,288},{96,384},{192,480},{288,576},{384,672},{480,0},{576,96},{6... | collective-permute-start | bytes 393224 | tf_op jit(solution)/shard_map/ppermute | solution.py:185
  80.6 4.3 %collective-permute-start.6 = (f32[64,512]{1,0:T(8,128)S(1)}, f32[64,512]{1,0:T(8,128)S(1)}, u32[]{:S(2)}, u32[]{:S(2)}) collective-permute-start(f32[64,512]{1,0:T(8,128)S(1)} %get-tuple-element.32), channel_id=1, source_target_pairs={{0,384},{96,480},{192,576},{288,672},{384,0},{480,96},{576,192},{6... | collective-permute-start | bytes 393224 | tf_op jit(solution)/shard_map/ppermute | solution.py:185
  84.8 3.5 %collective-permute-start.7 = (f32[64,512]{1,0:T(8,128)S(1)}, f32[64,512]{1,0:T(8,128)S(1)}, u32[]{:S(2)}, u32[]{:S(2)}) collective-permute-start(f32[64,512]{1,0:T(8,128)S(1)} %get-tuple-element.31), channel_id=1, source_target_pairs={{0,480},{96,576},{192,672},{288,0},{384,96},{480,192},{576,288},{6... | collective-permute-start | bytes 393224 | tf_op jit(solution)/shard_map/ppermute | solution.py:185
  89.7 9.6 %collective-permute-done.6.refs_4_ = f32[64,512]{1,0:T(8,128)S(1)} collective-permute-done((f32[64,512]{1,0:T(8,128)S(1)}, f32[64,512]{1,0:T(8,128)S(1)}, u32[]{:S(2)}, u32[]{:S(2)}) %collective-permute-start.6) | collective-permute-done | bytes 131104 | tf_op jit(solution)/shard_map/ppermute | solution.py:185
  99.4 10.6 %collective-permute-start.10 = (f32[16,1152]{1,0:T(8,128)S(1)}, f32[16,1152]{1,0:T(8,128)S(1)}, u32[]{:S(2)}, u32[]{:S(2)}) collective-permute-start(f32[16,1152]{1,0:T(8,128)S(1)} %add_select_fusion), channel_id=1, source_target_pairs={{0,16},{16,32},{32,0},{1,17},{17,33},{33,1},{2,18},{18,34},{34,2},... | collective-permute-start | bytes 221192 | tf_op jit(solution)/shard_map/ppermute | solution.py:190
  110.0 3.1 %collective-permute-start.11 = (f32[16,1152]{1,0:T(8,128)S(1)}, f32[16,1152]{1,0:T(8,128)S(1)}, u32[]{:S(2)}, u32[]{:S(2)}) collective-permute-start(f32[16,1152]{1,0:T(8,128)S(1)} %add_select_fusion), channel_id=1, source_target_pairs={{0,32},{16,0},{32,16},{1,33},{17,1},{33,17},{2,34},{18,2},{34,18},... | collective-permute-start | bytes 221192 | tf_op jit(solution)/shard_map/ppermute | solution.py:191
  113.8 8.4 %collective-permute-done.11 = f32[16,1152]{1,0:T(8,128)S(1)} collective-permute-done((f32[16,1152]{1,0:T(8,128)S(1)}, f32[16,1152]{1,0:T(8,128)S(1)}, u32[]{:S(2)}, u32[]{:S(2)}) %collective-permute-start.11) | collective-permute-done | bytes 73760 | tf_op jit(solution)/shard_map/ppermute | solution.py:191
  123.1 7.6 %all-to-all-start.2 = ((bf16[16,16,1152]{2,1,0:T(8,128)(2,1)}), bf16[16,16,1152]{2,1,0:T(8,128)(2,1)S(1)}, u32[]{:S(2)}, u32[]{:S(2)}) async-start(bf16[16,16,1152]{2,1,0:T(8,128)(2,1)} %broadcast_in_dim.10), calls=%async_computation.2 | async-start | bytes 1179648 | tf_op jit(solution)/shard_map/all_to_all | solution.py:44
  130.7 1.9 %collective-permute-start.2 = (f32[64,512]{1,0:T(8,128)S(1)}, f32[64,512]{1,0:T(8,128)S(1)}, u32[]{:S(2)}, u32[]{:S(2)}) collective-permute-start(f32[64,512]{1,0:T(8,128)S(1)} %get-tuple-element.35), channel_id=1, source_target_pairs={{0,96},{96,192},{192,288},{288,384},{384,480},{480,576},{576,672},... | collective-permute-start | bytes 393224 | tf_op jit(solution)/shard_map/ppermute | solution.py:185
  132.6 8.0 %collective-permute-start.8 = (f32[64,512]{1,0:T(8,128)S(1)}, f32[64,512]{1,0:T(8,128)S(1)}, u32[]{:S(2)}, u32[]{:S(2)}) collective-permute-start(f32[64,512]{1,0:T(8,128)S(1)} %get-tuple-element.30), channel_id=1, source_target_pairs={{0,576},{96,672},{192,0},{288,96},{384,192},{480,288},{576,384},{6... | collective-permute-start | bytes 393224 | tf_op jit(solution)/shard_map/ppermute | solution.py:185
  140.6 1.9 %collective-permute-start.9 = (f32[64,512]{1,0:T(8,128)S(1)}, f32[64,512]{1,0:T(8,128)S(1)}, u32[]{:S(2)}, u32[]{:S(2)}) collective-permute-start(f32[64,512]{1,0:T(8,128)S(1)} %get-tuple-element.29), channel_id=1, source_target_pairs={{0,672},{96,0},{192,96},{288,192},{384,288},{480,384},{576,480},{6... | collective-permute-start | bytes 393224 | tf_op jit(solution)/shard_map/ppermute | solution.py:185
  142.5 1.4 collective-permute-done.8.refs_6_
  143.9 3.5 %collective-permute-done.9.refs_7_ = f32[64,512]{1,0:T(8,128)S(1)} collective-permute-done((f32[64,512]{1,0:T(8,128)S(1)}, f32[64,512]{1,0:T(8,128)S(1)}, u32[]{:S(2)}, u32[]{:S(2)}) %collective-permute-start.9) | collective-permute-done | bytes 131104 | tf_op jit(solution)/shard_map/ppermute | solution.py:185
  147.4 1.2 shard_map.79
  (40 shorter events, 8.7 us)
Async XLA Ops:
  0.6 12.8 %copy-start.6 = (f32[256]{0:T(256)S(1)}, f32[256]{0:T(256)}, u32[]{:S(2)}) copy-start(f32[256]{0:T(256)} %param.9) | copy-start | bytes 3076
  0.7 1.0 copy-start
  1.7 0.9 copy-start.2
  2.6 0.7 copy-start.4
  3.3 8.2 %copy-start.5 = (bf16[256,1024]{1,0:T(8,128)(2,1)S(1)}, bf16[256,1024]{1,0:T(8,128)(2,1)}, u32[]{:S(2)}) copy-start(bf16[256,1024]{1,0:T(8,128)(2,1)} %mine_w.1) | copy-start | bytes 1572868
  3.3 12.6 %copy-start.3 = (bf16[1,64,1024]{2,1,0:T(8,128)(2,1)S(1)}, bf16[1,64,1024]{2,1,0:T(8,128)(2,1)}, u32[]{:S(2)}) copy-start(bf16[1,64,1024]{2,1,0:T(8,128)(2,1)} %param.6) | copy-start | bytes 393220
  4.4 48.6 %all-to-all-start = ((bf16[8,64,640]{2,1,0:T(8,128)(2,1)}), bf16[8,64,640]{2,1,0:T(8,128)(2,1)S(1)}, u32[]{:S(2)}, u32[]{:S(2)}) async-start(bf16[8,64,640]{2,1,0:T(8,128)(2,1)} %get-tuple-element.16), calls=%async_computation | async-start | bytes 1310720 | tf_op jit(solution)/shard_map/all_to_all | solution.py:44
  11.5 42.9 %collective-permute-start = (bf16[256,1024]{1,0:T(8,128)(2,1)S(1)}, bf16[256,1024]{1,0:T(8,128)(2,1)S(1)}, u32[]{:S(2)}, u32[]{:S(2)}) collective-permute-start(bf16[256,1024]{1,0:T(8,128)(2,1)S(1)} %copy-done.5), channel_id=1, source_target_pairs={{0,48},{48,0},{1,49},{49,1},{2,50},{50,2},{3,51},{51,3},{4,52},{52... | collective-permute-start | bytes 1572872 | tf_op jit(solution)/shard_map/ppermute | solution.py:164
  13.4 40.9 %collective-permute-start.1 = (f32[1,256]{1,0:T(1,128)S(1)}, f32[1,256]{1,0:T(1,128)S(1)}, u32[]{:S(2)}, u32[]{:S(2)}) collective-permute-start(f32[1,256]{1,0:T(1,128)S(1)} %bitcast.31), channel_id=1, source_target_pairs={{0,48},{48,0},{1,49},{49,1},{2,50},{50,2},{3,51},{51,3},{4,52},{52... | collective-permute-start | bytes 3080 | tf_op jit(solution)/shard_map/ppermute | solution.py:166
  55.9 4.6 %collective-permute-start.3 = (f32[264,1024]{1,0:T(8,128)S(1)}, f32[264,1024]{1,0:T(8,128)S(1)}, u32[]{:S(2)}, u32[]{:S(2)}) collective-permute-start(f32[264,1024]{1,0:T(8,128)S(1)} %get-tuple-element.19), channel_id=1, source_target_pairs={{0,48},{48,0},{1,49},{49,1},{2,50},{50,2},{3,51},{51,3},{4,52},{52... | collective-permute-start | bytes 3244040 | tf_op jit(solution)/shard_map/ppermute | solution.py:177
  61.5 26.9 %all-to-all-start.1 = ((bf16[16,16,1152]{2,1,0:T(8,128)(2,1)}), bf16[16,16,1152]{2,1,0:T(8,128)(2,1)S(1)}, u32[]{:S(2)}, u32[]{:S(2)}) async-start(bf16[16,16,1152]{2,1,0:T(8,128)(2,1)} %shard_map.78), calls=%async_computation.1 | async-start | bytes 1179648 | tf_op jit(solution)/shard_map/all_to_all | solution.py:44
  71.9 17.9 %collective-permute-start.4 = (f32[64,512]{1,0:T(8,128)S(1)}, f32[64,512]{1,0:T(8,128)S(1)}, u32[]{:S(2)}, u32[]{:S(2)}) collective-permute-start(f32[64,512]{1,0:T(8,128)S(1)} %get-tuple-element.34), channel_id=1, source_target_pairs={{0,192},{96,288},{192,384},{288,480},{384,576},{480,672},{576,0},{... | collective-permute-start | bytes 393224 | tf_op jit(solution)/shard_map/ppermute | solution.py:185
  75.2 14.6 %collective-permute-start.5 = (f32[64,512]{1,0:T(8,128)S(1)}, f32[64,512]{1,0:T(8,128)S(1)}, u32[]{:S(2)}, u32[]{:S(2)}) collective-permute-start(f32[64,512]{1,0:T(8,128)S(1)} %get-tuple-element.33), channel_id=1, source_target_pairs={{0,288},{96,384},{192,480},{288,576},{384,672},{480,0},{576,96},{6... | collective-permute-start | bytes 393224 | tf_op jit(solution)/shard_map/ppermute | solution.py:185
  80.6 18.8 %collective-permute-start.6 = (f32[64,512]{1,0:T(8,128)S(1)}, f32[64,512]{1,0:T(8,128)S(1)}, u32[]{:S(2)}, u32[]{:S(2)}) collective-permute-start(f32[64,512]{1,0:T(8,128)S(1)} %get-tuple-element.32), channel_id=1, source_target_pairs={{0,384},{96,480},{192,576},{288,672},{384,0},{480,96},{576,192},{6... | collective-permute-start | bytes 393224 | tf_op jit(solution)/shard_map/ppermute | solution.py:185
  84.8 14.6 %collective-permute-start.7 = (f32[64,512]{1,0:T(8,128)S(1)}, f32[64,512]{1,0:T(8,128)S(1)}, u32[]{:S(2)}, u32[]{:S(2)}) collective-permute-start(f32[64,512]{1,0:T(8,128)S(1)} %get-tuple-element.31), channel_id=1, source_target_pairs={{0,480},{96,576},{192,672},{288,0},{384,96},{480,192},{576,288},{6... | collective-permute-start | bytes 393224 | tf_op jit(solution)/shard_map/ppermute | solution.py:185
  99.4 14.4 %collective-permute-start.10 = (f32[16,1152]{1,0:T(8,128)S(1)}, f32[16,1152]{1,0:T(8,128)S(1)}, u32[]{:S(2)}, u32[]{:S(2)}) collective-permute-start(f32[16,1152]{1,0:T(8,128)S(1)} %add_select_fusion), channel_id=1, source_target_pairs={{0,16},{16,32},{32,0},{1,17},{17,33},{33,1},{2,18},{18,34},{34,2},... | collective-permute-start | bytes 221192 | tf_op jit(solution)/shard_map/ppermute | solution.py:190
  110.0 12.1 %collective-permute-start.11 = (f32[16,1152]{1,0:T(8,128)S(1)}, f32[16,1152]{1,0:T(8,128)S(1)}, u32[]{:S(2)}, u32[]{:S(2)}) collective-permute-start(f32[16,1152]{1,0:T(8,128)S(1)} %add_select_fusion), channel_id=1, source_target_pairs={{0,32},{16,0},{32,16},{1,33},{17,1},{33,17},{2,34},{18,2},{34,18},... | collective-permute-start | bytes 221192 | tf_op jit(solution)/shard_map/ppermute | solution.py:191
  113.2 34.3 %copy-start.1 = (bf16[1,64,4096]{2,1,0:T(8,128)(2,1)S(1)}, bf16[1,64,4096]{2,1,0:T(8,128)(2,1)}, u32[]{:S(2)}) copy-start(bf16[1,64,4096]{2,1,0:T(8,128)(2,1)} %param.5) | copy-start | bytes 1572868
  123.1 25.5 %all-to-all-start.2 = ((bf16[16,16,1152]{2,1,0:T(8,128)(2,1)}), bf16[16,16,1152]{2,1,0:T(8,128)(2,1)S(1)}, u32[]{:S(2)}, u32[]{:S(2)}) async-start(bf16[16,16,1152]{2,1,0:T(8,128)(2,1)} %broadcast_in_dim.10), calls=%async_computation.2 | async-start | bytes 1179648 | tf_op jit(solution)/shard_map/all_to_all | solution.py:44
  130.7 11.8 %collective-permute-start.2 = (f32[64,512]{1,0:T(8,128)S(1)}, f32[64,512]{1,0:T(8,128)S(1)}, u32[]{:S(2)}, u32[]{:S(2)}) collective-permute-start(f32[64,512]{1,0:T(8,128)S(1)} %get-tuple-element.35), channel_id=1, source_target_pairs={{0,96},{96,192},{192,288},{288,384},{384,480},{480,576},{576,672},... | collective-permute-start | bytes 393224 | tf_op jit(solution)/shard_map/ppermute | solution.py:185
  132.6 11.3 %collective-permute-start.8 = (f32[64,512]{1,0:T(8,128)S(1)}, f32[64,512]{1,0:T(8,128)S(1)}, u32[]{:S(2)}, u32[]{:S(2)}) collective-permute-start(f32[64,512]{1,0:T(8,128)S(1)} %get-tuple-element.30), channel_id=1, source_target_pairs={{0,576},{96,672},{192,0},{288,96},{384,192},{480,288},{576,384},{6... | collective-permute-start | bytes 393224 | tf_op jit(solution)/shard_map/ppermute | solution.py:185
  140.6 6.9 %collective-permute-start.9 = (f32[64,512]{1,0:T(8,128)S(1)}, f32[64,512]{1,0:T(8,128)S(1)}, u32[]{:S(2)}, u32[]{:S(2)}) collective-permute-start(f32[64,512]{1,0:T(8,128)S(1)} %get-tuple-element.29), channel_id=1, source_target_pairs={{0,672},{96,0},{192,96},{288,192},{384,288},{480,384},{576,480},{6... | collective-permute-start | bytes 393224 | tf_op jit(solution)/shard_map/ppermute | solution.py:185

commit v2 on v1

v2 whole, which is shorter than its diff:
```python
import jax
import jax.numpy as jnp
from jax import lax
from jax.experimental import pallas as pl
from jax.experimental.pallas import tpu as pltpu
from jax.sharding import Mesh
from jax.sharding import PartitionSpec as P

D = 4096
KVW = 1024
TOK_DEV = 256
ROWS = 64
EPS = 1e-05
LANES = 128
CHIPS = 8
OWN = D // CHIPS // 2
SHARES = 8
SHARE = OWN // SHARES
DEPTH = 3
STACK = 6
WIDE = KVW + LANES
PLANE = ("zl", "x")
PAIR = "zm"
DEEP = "zh"
SWAP = ((0, 1), (1, 0))
F32 = jnp.float32
BF16 = jnp.bfloat16
VMEM = pl.BlockSpec(memory_space=pltpu.VMEM)
SMEM = pl.BlockSpec(memory_space=pltpu.SMEM)


def call(kernel, n_scalars, outs, *args, flops=0, limit=24, scratch=(), spaces=None, out_space=pltpu.VMEM):
    shapes = [jax.ShapeDtypeStruct(shape, dtype) for shape, dtype in outs]
    sizes = [a.size * a.dtype.itemsize for a in (*args, *shapes)]
    return pl.pallas_call(
        kernel,
        out_shape=shapes,
        in_specs=[SMEM] * n_scalars + ([pl.BlockSpec(memory_space=space) for space in spaces] if spaces else [VMEM] * (len(args) - n_scalars)),
        out_specs=[pl.BlockSpec(memory_space=out_space)] * len(shapes),
        scratch_shapes=scratch,
        compiler_params=pltpu.CompilerParams(vmem_limit_bytes=int(limit * 2**20)),
        cost_estimate=pl.CostEstimate(flops=flops, bytes_accessed=sum(sizes), transcendentals=0),
    )(*args)


def rounded(value):
    return value.astype(BF16).astype(F32)


def exchange(blocks, axis):
    return lax.all_to_all(blocks, axis, 0, 0, tiled=True)


def prepare_kernel(first_ref, places_in, x_in, dv_in, slices_ref, inv_ref, places_ref, x_ref, dv_ref, arrived):
    copies = [
        pltpu.make_async_copy(x_in, x_ref, arrived.at[0]),
        pltpu.make_async_copy(dv_in, dv_ref, arrived.at[1]),
        pltpu.make_async_copy(places_in, places_ref, arrived.at[2]),
    ]
    for copy in copies:
        copy.start()
    for copy in copies:
        copy.wait()
    first = first_ref[0]
    places = places_ref[...]
    inside = jnp.where((places >= first) & (places < first + TOK_DEV), 1.0, 0.0)
    count = jnp.sum(inside, axis=1, keepdims=True)
    width = D // CHIPS
    squares = jnp.zeros((ROWS, LANES), F32)
    for j in range(CHIPS):
        block = x_ref[:, j * width:(j + 1) * width]
        slices_ref[j, :, :width] = block
        for k in range(0, width, LANES):
            part = block[:, k:k + LANES].astype(F32)
            squares = squares + part * part
    squares = jnp.sum(squares, axis=1, keepdims=True)
    row = lax.broadcasted_iota(jnp.int32, (ROWS, 1), 0).astype(F32)
    inv = jnp.where(row < count, lax.rsqrt(squares / D + EPS), 0.0)
    inv_ref[...] = jnp.broadcast_to(inv, (ROWS, LANES))
    high = rounded(inv)
    middle = rounded(inv - high)
    low = (inv - high) - middle
    lane = lax.broadcasted_iota(jnp.int32, (ROWS, LANES), 1)
    last = dv_ref[:, KVW - 1:].astype(F32)
    extra = jnp.where(lane == 0, last, jnp.where(lane == 1, high, jnp.where(lane == 2, middle, jnp.where(lane == 3, low, 0.0))))
    extra = extra.astype(BF16)
    for j in range(CHIPS):
        slices_ref[j, :, width:] = extra


def stack_kernel(other_ref, mine_ref, stack_ref, done):
    copies = [
        pltpu.make_async_copy(ref, stack_ref.at[i], done.at[i])
        for i, ref in enumerate((other_ref, mine_ref))
    ]
    for copy in copies:
        copy.start()
    for copy in copies:
        copy.wait()


def gain_lanes(high, rest, *others):
    row = lax.broadcasted_iota(jnp.int32, (SHARE, LANES), 0)
    extra = jnp.zeros((SHARE, LANES), F32)
    parts = (high[:, :LANES], high[:, LANES:], rest[:, :LANES], rest[:, LANES:], *others)
    for i, part in enumerate(parts):
        extra = jnp.where(row == i, part, extra)
    return extra


def gain_of(extra):
    return jnp.concatenate([extra[0:1] + extra[2:3], extra[1:2] + extra[3:4]], axis=1)


def products_kernel(
    core_ref, columns_ref, most_ref, weights_in, mine_g, other_g, back_out, blocks_out,
    weights_ref, dv_ref, back_ref, blocks_ref, arrived, left,
):
    copies = [
        pltpu.make_async_copy(weights_in.at[i], weights_ref.at[i], arrived.at[i]) for i in range(2)
    ]
    for copy in copies:
        copy.start()
    core = core_ref[0]
    width = D // CHIPS
    tail = KVW - LANES
    dv_ref[:, :tail] = most_ref[:, :tail]
    dv_ref[:, tail:KVW - 1] = most_ref[:, tail:]
    extra = columns_ref[:, :, width:].reshape(CHIPS * ROWS, LANES).astype(F32)
    inv = extra[:, 1:2] + extra[:, 2:3] + extra[:, 3:4]
    lane = lax.broadcasted_iota(jnp.int32, (CHIPS * ROWS, LANES), 1)
    ending = jnp.where(lane == LANES - 1, extra[:, 0:1], dv_ref[:, tail:].astype(F32))
    dv_ref[:, tail:] = ending.astype(BF16)
    dv = dv_ref[...]
    gained, largest, leaving = [], 0.0, []
    for i, (half, g_ref) in enumerate(((1 - core, other_g), (core, mine_g))):
        copies[i].wait()
        at = pl.multiple_of(half * OWN, OWN)
        dnormed = lax.dot_general(dv, weights_ref[i], (((1,), (1,)), ((), ())), preferred_element_type=F32)
        gain = g_ref[...]
        gained.append((at, dnormed * gain))
        largest = jnp.maximum(largest, jnp.max(jnp.abs(gained[-1][1]), axis=1, keepdims=True))
        normed = columns_ref[:, :, pl.ds(at, OWN)].reshape(CHIPS * ROWS, OWN).astype(F32) * inv
        scaled = (normed * gain).astype(BF16)
        weight = lax.dot_general(scaled, dv, (((0,), (0,)), ((), ())), preferred_element_type=F32)
        total = jnp.sum(dnormed * normed, axis=0, keepdims=True)
        high = rounded(total)
        mark = gain_lanes(high, total - high).astype(BF16)
        for j in range(SHARES):
            blocks_ref[i, j, :, :KVW] = weight[j * SHARE:(j + 1) * SHARE].astype(BF16)
            blocks_ref[i, j, :, KVW:] = mark
        leaving.append(pltpu.make_async_copy(blocks_ref.at[i], blocks_out.at[half], left.at[i]))
        leaving[-1].start()
    power = jnp.floor(jnp.log2(jnp.maximum(largest, 1e-30)))
    scale = jnp.exp2(-power)
    for at, value in gained:
        back_ref[:, :, pl.ds(at, OWN)] = (value * scale).reshape(CHIPS, ROWS, OWN)
    power = jnp.broadcast_to(power, (CHIPS * ROWS, LANES))
    back_ref[:, :, width:] = power.reshape(CHIPS, ROWS, LANES)
    leaving.append(pltpu.make_async_copy(back_ref, back_out, left.at[2]))
    leaving[-1].start()
    for copy in leaving:
        copy.wait()


def exponent(value):
    largest = jnp.max(jnp.max(jnp.abs(value), axis=1, keepdims=True), axis=0, keepdims=True)
    return jnp.floor(jnp.log2(jnp.maximum(largest, 1e-30)))


def pack(weight, gain, part_ref):
    weight_power, gain_power = exponent(weight), exponent(gain)
    part_ref[:, :KVW] = weight * jnp.exp2(-weight_power)
    gain = gain * jnp.exp2(-gain_power)
    high = rounded(gain)
    wide = [jnp.broadcast_to(power, (1, LANES)) for power in (weight_power, gain_power)]
    part_ref[:, KVW:] = gain_lanes(high, gain - high, *wide)


def unpack(part):
    extra = part[:, KVW:]
    return part[:, :KVW] * jnp.exp2(extra[4:5, :1]), gain_of(extra) * jnp.exp2(extra[5:6, :1])


def partial_kernel(blocks_ref, part_ref):
    total = blocks_ref[0].astype(F32)
    for i in range(1, 2 * SHARES):
        total = total + blocks_ref[i].astype(F32)
    pack(total[:, :KVW], gain_of(total[:, KVW:]), part_ref)


def pair_kernel(mine_ref, theirs_ref, part_ref):
    (weight, gain), (more_weight, more_gain) = unpack(mine_ref[...]), unpack(theirs_ref[...])
    pack(weight + more_weight, gain + more_gain, part_ref)


def total_kernel(me_ref, *refs):
    parts, out_ref, held_ref = refs[:DEPTH], refs[-2], refs[-1]
    me = me_ref[0]
    for k, part in enumerate(parts):
        held_ref[lax.rem(me + DEPTH - k, DEPTH)] = part[...]
    weight, gain = unpack(held_ref[0])
    for i in range(1, DEPTH):
        more_weight, more_gain = unpack(held_ref[i])
        weight, gain = weight + more_weight, gain + more_gain
    weight = weight.astype(BF16)
    high = rounded(gain)
    mark = gain_lanes(high, gain - high).astype(BF16)
    for j in range(SHARES):
        out_ref[j, :, :KVW] = weight
        out_ref[j, :, KVW:] = mark


def finish_kernel(whole_ref, w_ref, g_ref):
    for j in range(SHARES):
        w_ref[j * SHARE:(j + 1) * SHARE, :] = whole_ref[j, :, :KVW].astype(F32)
    g_ref[...] = gain_of(whole_ref[0, :, KVW:].astype(F32))


def rows_kernel(x_ref, inv_ref, back_ref, out_ref):
    width = D // CHIPS
    total = jnp.zeros((ROWS, LANES), F32)
    scales = [jnp.exp2(back_ref[j, :, width:width + 1]) for j in range(CHIPS)]
    for j, scale in enumerate(scales):
        product = back_ref[j, :, :width] * x_ref[:, j * width:(j + 1) * width].astype(F32)
        part = product[:, :LANES]
        for k in range(LANES, width, LANES):
            part = part + product[:, k:k + LANES]
        total = total + part * scale
    inv = inv_ref[:, :1]
    mean = inv * (jnp.sum(total, axis=1, keepdims=True) / D)
    shift = inv * mean
    for j, scale in enumerate(scales):
        at = slice(j * width, (j + 1) * width)
        values = x_ref[:, at].astype(F32)
        out_ref[:, at] = (inv * (back_ref[j, :, :width] * scale - values * shift)).astype(BF16)


def body(sel_inputs, val_grads, positions, value_weight, norm_gain):
    inputs, grads = sel_inputs[0], val_grads[0]
    chip, core = lax.axis_index("y"), lax.axis_index("core")
    first = ((chip * 2 + core) * TOK_DEV).reshape(1)
    width = D // CHIPS
    gain = norm_gain.reshape(1, OWN)
    slices, inv = call(
        prepare_kernel, 1,
        [((CHIPS, ROWS, width + LANES), BF16), ((ROWS, LANES), F32)],
        first, positions, inputs, grads,
        spaces=[pltpu.HBM] * 3, limit=56,
        scratch=[
            pltpu.VMEM(positions.shape, jnp.int32), pltpu.VMEM((ROWS, D), BF16),
            pltpu.VMEM((ROWS, KVW), BF16), pltpu.SemaphoreType.DMA((3,)),
        ],
    )
    columns = exchange(slices, "y")
    other_weight = lax.ppermute(value_weight, "core", SWAP)
    other_gain = lax.ppermute(gain, "core", SWAP)
    (weights,) = call(
        stack_kernel, 0, [((STACK, OWN, KVW), BF16)], other_weight, value_weight,
        spaces=[pltpu.HBM] * 2, out_space=pltpu.HBM, scratch=[pltpu.SemaphoreType.DMA((2,))],
    )
    grads, weights = lax.optimization_barrier((grads, weights))
    most = lax.all_gather(grads[:, :KVW - 1], "y", axis=0, tiled=True)

    back, blocks = call(
        products_kernel, 1,
        [((CHIPS, ROWS, width + LANES), F32), ((2, SHARES, SHARE, WIDE), BF16)],
        core.reshape(1), columns, most, weights, gain, other_gain,
        spaces=[pltpu.VMEM] * 2 + [pltpu.HBM] + [pltpu.VMEM] * 2, out_space=pltpu.HBM, limit=52,
        flops=4 * CHIPS * ROWS * width * KVW,
        scratch=[
            pltpu.VMEM((2, OWN, KVW), BF16), pltpu.VMEM((CHIPS * ROWS, KVW), BF16),
            pltpu.VMEM((CHIPS, ROWS, width + LANES), F32), pltpu.VMEM((2, SHARES, SHARE, WIDE), BF16),
            pltpu.SemaphoreType.DMA((2,)), pltpu.SemaphoreType.DMA((3,)),
        ],
    )
    blocks = exchange(blocks.reshape(2 * SHARES, SHARE, WIDE), ("core", *PLANE))
    (part,) = call(partial_kernel, 0, [((SHARE, WIDE), F32)], blocks)

    part, back = lax.optimization_barrier((part.astype(jnp.float16), back.astype(jnp.float16)))
    back = exchange(back, "y")
    theirs = lax.ppermute(part, PAIR, SWAP)
    (part,) = call(pair_kernel, 0, [((SHARE, WIDE), F32)], part.astype(F32), theirs.astype(F32))
    part = lax.optimization_barrier(part.astype(jnp.float16))
    parts = [part] + [
        lax.ppermute(part, DEEP, [(i, (i + k) % DEPTH) for i in range(DEPTH)])
        for k in range(1, DEPTH)
    ]
    (whole,) = call(
        total_kernel, 1, [((SHARES, SHARE, WIDE), BF16)],
        lax.axis_index(DEEP).reshape(1), *[part.astype(F32) for part in parts],
        scratch=[pltpu.VMEM((DEPTH, SHARE, WIDE), F32)],
    )
    whole, back = lax.optimization_barrier((whole, back))
    whole = exchange(whole, PLANE)

    (result,) = call(rows_kernel, 0, [((ROWS, D), BF16)], inputs, inv, back.astype(F32))
    weight_grad, gain_grad = call(
        finish_kernel, 0, [((OWN, KVW), F32), ((1, OWN), F32)], whole
    )
    return result[None], weight_grad, gain_grad.reshape(OWN)


def solution(mesh):
    fine = Mesh(
        mesh.devices.reshape(8, 2, 3, 2, 2, 4), ("y", "core", "zh", "zm", "zl", "x")
    )
    seq, fsdp = ("y", "core"), ("zh", "zm", "zl", "x")
    return jax.shard_map(
        body,
        mesh=fine,
        in_specs=(P(fsdp, seq, None), P(fsdp, seq, None), P(fsdp, None), P(seq, None), P(seq)),
        out_specs=(P(fsdp, seq, None), P(seq, None), P(seq)),
        check_vma=False,
    )
```

time: 151 us -> 131 us (0.87)
  the two profiles are of different devices: /device:TPU:2 before, /device:TPU:8 now
where the time goes in v2:
time: 131 us
  starting transfers between devices  52.9 us (40%)
  waiting for transfers between devices  36.9 us (28%)
  blocking collectives  27.4 us (21%)
  Pallas kernels  10 us (8%)
  local copies, waits for them, and re-layouts  1.66 us (1%)
    all_to_all x4, starting transfers between devices, exchange(): return lax.all_to_all(blocks, axis, 0, 0, tiled=True)  28.4 us
    all_gather x1, blocking collectives, body(): most = lax.all_gather(grads[:, :KVW - 1], 'y', axis=0, tiled=True)  27.4 us
    all_to_all x4, waiting for transfers between devices, exchange(): return lax.all_to_all(blocks, axis, 0, 0, tiled=True)  23.9 us
    ppermute x2, starting transfers between devices, body(): lax.ppermute(part, DEEP, [(i, (i + k) % DEPTH) for i in range(DEPTH)])  14 us
    pallas_call x8, Pallas kernels, call(): pl.pallas_call(kernel, out_shape=shapes, in_specs=[SMEM] * n_scalars + ([...  10 us
    ppermute x2, waiting for transfers between devices, body(): lax.ppermute(part, DEEP, [(i, (i + k) % DEPTH) for i in range(DEPTH)])  9.49 us
    ppermute x1, starting transfers between devices, body(): theirs = lax.ppermute(part, PAIR, SWAP)  6.08 us
    ppermute x1, waiting for transfers between devices, body(): theirs = lax.ppermute(part, PAIR, SWAP)  3.53 us
  transfers between devices with their start and end apart: 9, of which 5 were waited for; matrix products, arithmetic and copies ran while one was open for 1% of the time, Pallas kernels for 2%

profile of v2, /device:TPU:8, one launch (start us, length us, event | category | flops | bytes accessed | tf_op | source)
XLA Modules:
  0.0 130.9 jit_solution(16311111468499583302)
XLA Ops:
  0.7 2.2 %shard_map.76 = (bf16[8,64,640]{2,1,0:T(8,128)(2,1)}, f32[64,128]{1,0:T(8,128)}) custom-call(s32[1]{0:T(128)} %bitcast.1.first_ref, s32[1,512]{1,0:T(1,128)} %places_in.1, bf16[64,4096]{1,0:T(8,128)(2,1)} %bitcast.10, bf16[64,1024]{1,0:T(8,128)(2,1)} %bitcast.15), custom_call_target="tpu_custom_call" | custom-call | bytes 1345540 | tf_op jit(solution)/shard_map/pallas_call | solution.py:35
  2.9 12.9 %all-to-all-start = ((bf16[8,64,640]{2,1,0:T(8,128)(2,1)}), bf16[8,64,640]{2,1,0:T(8,128)(2,1)S(1)}, u32[]{:S(2)}, u32[]{:S(2)}) async-start(bf16[8,64,640]{2,1,0:T(8,128)(2,1)} %get-tuple-element.16), calls=%async_computation | async-start | bytes 1310720 | tf_op jit(solution)/shard_map/all_to_all | solution.py:51
  15.8 1.9 %collective-permute-start = (bf16[256,1024]{1,0:T(8,128)(2,1)S(1)}, bf16[256,1024]{1,0:T(8,128)(2,1)S(1)}, u32[]{:S(2)}, u32[]{:S(2)}) collective-permute-start(bf16[256,1024]{1,0:T(8,128)(2,1)S(1)} %copy-done.2), channel_id=1, source_target_pairs={{0,48},{48,0},{1,49},{49,1},{2,50},{50,2},{3,51},{51,3},{4,52},{52... | collective-permute-start | bytes 1572872 | tf_op jit(solution)/shard_map/ppermute | solution.py:256
  17.8 2.5 %collective-permute-start.1 = (f32[1,256]{1,0:T(1,128)S(1)}, f32[1,256]{1,0:T(1,128)S(1)}, u32[]{:S(2)}, u32[]{:S(2)}) collective-permute-start(f32[1,256]{1,0:T(1,128)S(1)} %bitcast.12), channel_id=1, source_target_pairs={{0,48},{48,0},{1,49},{49,1},{2,50},{50,2},{3,51},{51,3},{4,52},{52... | collective-permute-start | bytes 3080 | tf_op jit(solution)/shard_map/ppermute | solution.py:257
  20.4 1.6 %copy-done = bf16[6,256,1024]{2,1,0:T(8,128)(2,1)} copy-done((bf16[6,256,1024]{2,1,0:T(8,128)(2,1)}, bf16[6,256,1024]{2,1,0:T(8,128)(2,1)S(1)}, u32[]{:S(2)}) %copy-start) | copy-done | bytes 3145752
  22.1 27.4 %all_gather.3.most_ref = bf16[512,1023]{1,0:T(8,128)(2,1)S(1)} all-gather(bf16[64,1023]{1,0:T(8,128)(2,1)S(1)} %bitcast.16), channel_id=1, replica_groups=mesh['y'=8,'core'=2,'zh'=3,'zm'=2,'zl'=2,'x'=4] {'y'}, dimensions={0}, use_global_device_ids=true | all-gather | bytes 1178496 | tf_op jit(solution)/shard_map/all_gather | solution.py:263
  49.4 4.0 %shard_map.78 = (f32[8,64,640]{2,1,0:T(8,128)}, bf16[2,8,32,1152]{3,2,1,0:T(8,128)(2,1)}) custom-call(s32[1]{0:T(128)} %bitcast.4.core_ref, bf16[8,64,640]{2,1,0:T(8,128)(2,1)S(1)} %all-to-all-done.columns_ref, bf16[512,1023]{1,0:T(8,128)(2,1)S(1)} %all_gather.3.most_ref, bf16[6,256,1024]{2,1,0:T(8,128)(2,1)} %copy-done, f32[1,256]{1,0:T(1,128)S(1)} %bitcast.13, ...), custom_call_target="tpu_custom_call" | custom-call | flops 1073741824 | bytes 7341060 | tf_op jit(solution)/shard_map/pallas_call | solution.py:35
  53.5 6.4 %all-to-all-start.1 = ((bf16[16,32,1152]{2,1,0:T(8,128)(2,1)}), bf16[16,32,1152]{2,1,0:T(8,128)(2,1)S(1)}, u32[]{:S(2)}, u32[]{:S(2)}) async-start(bf16[16,32,1152]{2,1,0:T(8,128)(2,1)} %bitcast.14), calls=%async_computation.1 | async-start | bytes 2359296 | tf_op jit(solution)/shard_map/all_to_all | solution.py:51
  59.8 0.9 convert_element_type.28
  60.8 16.8 %all-to-all-done.1.blocks_ref = bf16[16,32,1152]{2,1,0:T(8,128)(2,1)S(1)} async-done(((bf16[16,32,1152]{2,1,0:T(8,128)(2,1)}), bf16[16,32,1152]{2,1,0:T(8,128)(2,1)S(1)}, u32[]{:S(2)}, u32[]{:S(2)}) %all-to-all-start.1) | async-done | bytes 1179680 | tf_op jit(solution)/shard_map/all_to_all | solution.py:51
  77.5 0.3 shard_map.79
  77.8 5.4 %all-to-all-start.2 = ((f16[8,64,640]{2,1,0:T(8,128)(2,1)}), f16[8,64,640]{2,1,0:T(8,128)(2,1)S(1)}, u32[]{:S(2)}, u32[]{:S(2)}) async-start(f16[8,64,640]{2,1,0:T(8,128)(2,1)} %convert_element_type.28), calls=%async_computation.2 | async-start | bytes 1310720 | tf_op jit(solution)/shard_map/all_to_all | solution.py:51
  83.2 6.1 %collective-permute-start.2 = (f16[32,1152]{1,0:T(8,128)(2,1)S(1)}, f16[32,1152]{1,0:T(8,128)(2,1)S(1)}, u32[]{:S(2)}, u32[]{:S(2)}) collective-permute-start(f16[32,1152]{1,0:T(8,128)(2,1)S(1)} %convert_element_type.27), channel_id=1, source_target_pairs={{0,8},{8,0},{1,9},{9,1},{2,10},{10,2},{3,11},{11,3},{4,12},{12,4},... | collective-permute-start | bytes 221192 | tf_op jit(solution)/shard_map/ppermute | solution.py:282
  89.3 3.5 %collective-permute-done.2 = f16[32,1152]{1,0:T(8,128)(2,1)S(1)} collective-permute-done((f16[32,1152]{1,0:T(8,128)(2,1)S(1)}, f16[32,1152]{1,0:T(8,128)(2,1)S(1)}, u32[]{:S(2)}, u32[]{:S(2)}) %collective-permute-start.2) | collective-permute-done | bytes 73760 | tf_op jit(solution)/shard_map/ppermute | solution.py:282
  92.9 0.2 shard_map.80
  93.1 12.1 %collective-permute-start.4 = (f16[32,1152]{1,0:T(8,128)(2,1)S(1)}, f16[32,1152]{1,0:T(8,128)(2,1)S(1)}, u32[]{:S(2)}, u32[]{:S(2)}) collective-permute-start(f16[32,1152]{1,0:T(8,128)(2,1)S(1)} %convert_element_type.31), channel_id=1, source_target_pairs={{0,32},{16,0},{32,16},{1,33},{17,1},{33,17},{2,34},{18,2},{34,18},... | collective-permute-start | bytes 221192 | tf_op jit(solution)/shard_map/ppermute | solution.py:286
  105.2 1.9 %collective-permute-start.3 = (f16[32,1152]{1,0:T(8,128)(2,1)S(1)}, f16[32,1152]{1,0:T(8,128)(2,1)S(1)}, u32[]{:S(2)}, u32[]{:S(2)}) collective-permute-start(f16[32,1152]{1,0:T(8,128)(2,1)S(1)} %convert_element_type.31), channel_id=1, source_target_pairs={{0,16},{16,32},{32,0},{1,17},{17,33},{33,1},{2,18},{18,34},{34,2},... | collective-permute-start | bytes 221192 | tf_op jit(solution)/shard_map/ppermute | solution.py:286
  107.2 2.7 %collective-permute-done.4 = f16[32,1152]{1,0:T(8,128)(2,1)S(1)} collective-permute-done((f16[32,1152]{1,0:T(8,128)(2,1)S(1)}, f16[32,1152]{1,0:T(8,128)(2,1)S(1)}, u32[]{:S(2)}, u32[]{:S(2)}) %collective-permute-start.4) | collective-permute-done | bytes 73760 | tf_op jit(solution)/shard_map/ppermute | solution.py:286
  109.8 6.8 %collective-permute-done.3 = f16[32,1152]{1,0:T(8,128)(2,1)S(1)} collective-permute-done((f16[32,1152]{1,0:T(8,128)(2,1)S(1)}, f16[32,1152]{1,0:T(8,128)(2,1)S(1)}, u32[]{:S(2)}, u32[]{:S(2)}) %collective-permute-start.3) | collective-permute-done | bytes 73760 | tf_op jit(solution)/shard_map/ppermute | solution.py:286
  116.7 1.0 shard_map.81
  117.7 3.7 %all-to-all-start.3 = ((bf16[8,32,1152]{2,1,0:T(8,128)(2,1)}), bf16[8,32,1152]{2,1,0:T(8,128)(2,1)S(1)}, u32[]{:S(2)}, u32[]{:S(2)}) async-start(bf16[8,32,1152]{2,1,0:T(8,128)(2,1)} %shard_map.81), calls=%async_computation.3 | async-start | bytes 1179648 | tf_op jit(solution)/shard_map/all_to_all | solution.py:51
  121.5 1.3 shard_map.82
  122.7 7.1 %all-to-all-done.3.whole_ref = bf16[8,32,1152]{2,1,0:T(8,128)(2,1)S(1)} async-done(((bf16[8,32,1152]{2,1,0:T(8,128)(2,1)}), bf16[8,32,1152]{2,1,0:T(8,128)(2,1)S(1)}, u32[]{:S(2)}, u32[]{:S(2)}) %all-to-all-start.3) | async-done | bytes 589856 | tf_op jit(solution)/shard_map/all_to_all | solution.py:51
  129.8 1.0 shard_map.83
  (26 shorter events, 0.3 us)
Async XLA Ops:
  0.6 15.2 %copy-start.2 = (bf16[256,1024]{1,0:T(8,128)(2,1)S(1)}, bf16[256,1024]{1,0:T(8,128)(2,1)}, u32[]{:S(2)}) copy-start(bf16[256,1024]{1,0:T(8,128)(2,1)} %mine_ref.1) | copy-start | bytes 1572868
  0.6 17.1 %copy-start.4 = (f32[256]{0:T(256)S(1)}, f32[256]{0:T(256)}, u32[]{:S(2)}) copy-start(f32[256]{0:T(256)} %param.9) | copy-start | bytes 3076
  2.9 46.5 %all-to-all-start = ((bf16[8,64,640]{2,1,0:T(8,128)(2,1)}), bf16[8,64,640]{2,1,0:T(8,128)(2,1)S(1)}, u32[]{:S(2)}, u32[]{:S(2)}) async-start(bf16[8,64,640]{2,1,0:T(8,128)(2,1)} %get-tuple-element.16), calls=%async_computation | async-start | bytes 1310720 | tf_op jit(solution)/shard_map/all_to_all | solution.py:51
  15.8 4.5 %collective-permute-start = (bf16[256,1024]{1,0:T(8,128)(2,1)S(1)}, bf16[256,1024]{1,0:T(8,128)(2,1)S(1)}, u32[]{:S(2)}, u32[]{:S(2)}) collective-permute-start(bf16[256,1024]{1,0:T(8,128)(2,1)S(1)} %copy-done.2), channel_id=1, source_target_pairs={{0,48},{48,0},{1,49},{49,1},{2,50},{50,2},{3,51},{51,3},{4,52},{52... | collective-permute-start | bytes 1572872 | tf_op jit(solution)/shard_map/ppermute | solution.py:256
  17.7 4.3 %copy-start.6 = (bf16[1,64,1024]{2,1,0:T(8,128)(2,1)S(1)}, bf16[1,64,1024]{2,1,0:T(8,128)(2,1)}, u32[]{:S(2)}) copy-start(bf16[1,64,1024]{2,1,0:T(8,128)(2,1)} %param.6) | copy-start | bytes 393220
  17.8 31.7 %collective-permute-start.1 = (f32[1,256]{1,0:T(1,128)S(1)}, f32[1,256]{1,0:T(1,128)S(1)}, u32[]{:S(2)}, u32[]{:S(2)}) collective-permute-start(f32[1,256]{1,0:T(1,128)S(1)} %bitcast.12), channel_id=1, source_target_pairs={{0,48},{48,0},{1,49},{49,1},{2,50},{50,2},{3,51},{51,3},{4,52},{52... | collective-permute-start | bytes 3080 | tf_op jit(solution)/shard_map/ppermute | solution.py:257
  20.4 1.6 %copy-start = (bf16[6,256,1024]{2,1,0:T(8,128)(2,1)}, bf16[6,256,1024]{2,1,0:T(8,128)(2,1)S(1)}, u32[]{:S(2)}) copy-start(bf16[6,256,1024]{2,1,0:T(8,128)(2,1)S(1)} %shard_map.77.weights_in) | copy-start | bytes 9437188
  53.5 6.4 %copy-start.5 = (f32[8,64,640]{2,1,0:T(8,128)S(1)}, f32[8,64,640]{2,1,0:T(8,128)}, u32[]{:S(2)}) copy-start(f32[8,64,640]{2,1,0:T(8,128)} %get-tuple-element.20) | copy-start | bytes 3932164
  53.5 24.1 %all-to-all-start.1 = ((bf16[16,32,1152]{2,1,0:T(8,128)(2,1)}), bf16[16,32,1152]{2,1,0:T(8,128)(2,1)S(1)}, u32[]{:S(2)}, u32[]{:S(2)}) async-start(bf16[16,32,1152]{2,1,0:T(8,128)(2,1)} %bitcast.14), calls=%async_computation.1 | async-start | bytes 2359296 | tf_op jit(solution)/shard_map/all_to_all | solution.py:51
  77.8 39.8 %all-to-all-start.2 = ((f16[8,64,640]{2,1,0:T(8,128)(2,1)}), f16[8,64,640]{2,1,0:T(8,128)(2,1)S(1)}, u32[]{:S(2)}, u32[]{:S(2)}) async-start(f16[8,64,640]{2,1,0:T(8,128)(2,1)} %convert_element_type.28), calls=%async_computation.2 | async-start | bytes 1310720 | tf_op jit(solution)/shard_map/all_to_all | solution.py:51
  83.2 9.6 %collective-permute-start.2 = (f16[32,1152]{1,0:T(8,128)(2,1)S(1)}, f16[32,1152]{1,0:T(8,128)(2,1)S(1)}, u32[]{:S(2)}, u32[]{:S(2)}) collective-permute-start(f16[32,1152]{1,0:T(8,128)(2,1)S(1)} %convert_element_type.27), channel_id=1, source_target_pairs={{0,8},{8,0},{1,9},{9,1},{2,10},{10,2},{3,11},{11,3},{4,12},{12,4},... | collective-permute-start | bytes 221192 | tf_op jit(solution)/shard_map/ppermute | solution.py:282
  93.1 16.7 %collective-permute-start.4 = (f16[32,1152]{1,0:T(8,128)(2,1)S(1)}, f16[32,1152]{1,0:T(8,128)(2,1)S(1)}, u32[]{:S(2)}, u32[]{:S(2)}) collective-permute-start(f16[32,1152]{1,0:T(8,128)(2,1)S(1)} %convert_element_type.31), channel_id=1, source_target_pairs={{0,32},{16,0},{32,16},{1,33},{17,1},{33,17},{2,34},{18,2},{34,18},... | collective-permute-start | bytes 221192 | tf_op jit(solution)/shard_map/ppermute | solution.py:286
  105.2 11.5 %collective-permute-start.3 = (f16[32,1152]{1,0:T(8,128)(2,1)S(1)}, f16[32,1152]{1,0:T(8,128)(2,1)S(1)}, u32[]{:S(2)}, u32[]{:S(2)}) collective-permute-start(f16[32,1152]{1,0:T(8,128)(2,1)S(1)} %convert_element_type.31), channel_id=1, source_target_pairs={{0,16},{16,32},{32,0},{1,17},{17,33},{33,1},{2,18},{18,34},{34,2},... | collective-permute-start | bytes 221192 | tf_op jit(solution)/shard_map/ppermute | solution.py:286
  117.7 3.8 %copy-start.1 = (bf16[1,64,4096]{2,1,0:T(8,128)(2,1)S(1)}, bf16[1,64,4096]{2,1,0:T(8,128)(2,1)}, u32[]{:S(2)}) copy-start(bf16[1,64,4096]{2,1,0:T(8,128)(2,1)} %param.5) | copy-start | bytes 1572868
  117.7 3.8 %copy-start.3 = (f32[64,128]{1,0:T(8,128)S(1)}, f32[64,128]{1,0:T(8,128)}, u32[]{:S(2)}) copy-start(f32[64,128]{1,0:T(8,128)} %get-tuple-element.15.inv_ref) | copy-start | bytes 98308
  117.7 12.2 %all-to-all-start.3 = ((bf16[8,32,1152]{2,1,0:T(8,128)(2,1)}), bf16[8,32,1152]{2,1,0:T(8,128)(2,1)S(1)}, u32[]{:S(2)}, u32[]{:S(2)}) async-start(bf16[8,32,1152]{2,1,0:T(8,128)(2,1)} %shard_map.81), calls=%async_computation.3 | async-start | bytes 1179648 | tf_op jit(solution)/shard_map/all_to_all | solution.py:51

commit v3 on v2

--- a/solution.py
+++ b/solution.py
@@ -16,12 +16,11 @@
 OWN = D // CHIPS // 2
 SHARES = 8
 SHARE = OWN // SHARES
-DEPTH = 3
+DEPTH = 6
 STACK = 6
-WIDE = KVW + LANES
+TALL = 256 + 16
 PLANE = ("zl", "x")
-PAIR = "zm"
-DEEP = "zh"
+DEEP = ("zh", "zm")
 SWAP = ((0, 1), (1, 0))
 F32 = jnp.float32
 BF16 = jnp.bfloat16
@@ -99,9 +98,9 @@
         copy.wait()
 
 
-def gain_lanes(high, rest, *others):
-    row = lax.broadcasted_iota(jnp.int32, (SHARE, LANES), 0)
-    extra = jnp.zeros((SHARE, LANES), F32)
+def gain_rows(high, rest, *others):
+    row = lax.broadcasted_iota(jnp.int32, (16, LANES), 0)
+    extra = jnp.zeros((16, LANES), F32)
     parts = (high[:, :LANES], high[:, LANES:], rest[:, :LANES], rest[:, LANES:], *others)
     for i, part in enumerate(parts):
         extra = jnp.where(row == i, part, extra)
@@ -135,20 +134,22 @@
     gained, largest, leaving = [], 0.0, []
     for i, (half, g_ref) in enumerate(((1 - core, other_g), (core, mine_g))):
         copies[i].wait()
-        at = pl.multiple_of(half * OWN, OWN)
+        gain = g_ref[...]
         dnormed = lax.dot_general(dv, weights_ref[i], (((1,), (1,)), ((), ())), preferred_element_type=F32)
-        gain = g_ref[...]
-        gained.append((at, dnormed * gain))
+        gained.append((pl.multiple_of(half * OWN, OWN), dnormed * gain))
         largest = jnp.maximum(largest, jnp.max(jnp.abs(gained[-1][1]), axis=1, keepdims=True))
+        at = gained[-1][0]
         normed = columns_ref[:, :, pl.ds(at, OWN)].reshape(CHIPS * ROWS, OWN).astype(F32) * inv
         scaled = (normed * gain).astype(BF16)
         weight = lax.dot_general(scaled, dv, (((0,), (0,)), ((), ())), preferred_element_type=F32)
         total = jnp.sum(dnormed * normed, axis=0, keepdims=True)
         high = rounded(total)
-        mark = gain_lanes(high, total - high).astype(BF16)
+        mark = gain_rows(high, total - high).astype(BF16)
         for j in range(SHARES):
-            blocks_ref[i, j, :, :KVW] = weight[j * SHARE:(j + 1) * SHARE].astype(BF16)
-            blocks_ref[i, j, :, KVW:] = mark
+            rows = weight[j * SHARE:(j + 1) * SHARE].astype(BF16)
+            for k in range(KVW // LANES):
+                blocks_ref[i, j, k * SHARE:(k + 1) * SHARE, :] = rows[:, k * LANES:(k + 1) * LANES]
+            blocks_ref[i, j, 256:, :] = mark
         leaving.append(pltpu.make_async_copy(blocks_ref.at[i], blocks_out.at[half], left.at[i]))
         leaving[-1].start()
     power = jnp.floor(jnp.log2(jnp.maximum(largest, 1e-30)))
@@ -170,51 +171,44 @@
 
 def pack(weight, gain, part_ref):
     weight_power, gain_power = exponent(weight), exponent(gain)
-    part_ref[:, :KVW] = weight * jnp.exp2(-weight_power)
+    part_ref[:256, :] = weight * jnp.exp2(-weight_power)
     gain = gain * jnp.exp2(-gain_power)
     high = rounded(gain)
     wide = [jnp.broadcast_to(power, (1, LANES)) for power in (weight_power, gain_power)]
-    part_ref[:, KVW:] = gain_lanes(high, gain - high, *wide)
+    part_ref[256:, :] = gain_rows(high, gain - high, *wide)
 
 
 def unpack(part):
-    extra = part[:, KVW:]
-    return part[:, :KVW] * jnp.exp2(extra[4:5, :1]), gain_of(extra) * jnp.exp2(extra[5:6, :1])
+    extra = part[256:]
+    return part[:256] * jnp.exp2(extra[4:5, :1]), gain_of(extra) * jnp.exp2(extra[5:6, :1])
 
 
 def partial_kernel(blocks_ref, part_ref):
     total = blocks_ref[0].astype(F32)
     for i in range(1, 2 * SHARES):
         total = total + blocks_ref[i].astype(F32)
-    pack(total[:, :KVW], gain_of(total[:, KVW:]), part_ref)
-
-
-def pair_kernel(mine_ref, theirs_ref, part_ref):
-    (weight, gain), (more_weight, more_gain) = unpack(mine_ref[...]), unpack(theirs_ref[...])
-    pack(weight + more_weight, gain + more_gain, part_ref)
-
-
-def total_kernel(me_ref, *refs):
-    parts, out_ref, held_ref = refs[:DEPTH], refs[-2], refs[-1]
-    me = me_ref[0]
-    for k, part in enumerate(parts):
-        held_ref[lax.rem(me + DEPTH - k, DEPTH)] = part[...]
-    weight, gain = unpack(held_ref[0])
+    pack(total[:256], gain_of(total[256:]), part_ref)
+
+
+def total_kernel(parts_ref, out_ref):
+    weight, gain = unpack(parts_ref[0])
     for i in range(1, DEPTH):
-        more_weight, more_gain = unpack(held_ref[i])
+        more_weight, more_gain = unpack(parts_ref[i])
         weight, gain = weight + more_weight, gain + more_gain
     weight = weight.astype(BF16)
     high = rounded(gain)
-    mark = gain_lanes(high, gain - high).astype(BF16)
+    mark = gain_rows(high, gain - high).astype(BF16)
     for j in range(SHARES):
-        out_ref[j, :, :KVW] = weight
-        out_ref[j, :, KVW:] = mark
+        out_ref[j, :256, :] = weight
+        out_ref[j, 256:, :] = mark
 
 
 def finish_kernel(whole_ref, w_ref, g_ref):
     for j in range(SHARES):
-        w_ref[j * SHARE:(j + 1) * SHARE, :] = whole_ref[j, :, :KVW].astype(F32)
-    g_ref[...] = gain_of(whole_ref[0, :, KVW:].astype(F32))
+        for k in range(KVW // LANES):
+            part = whole_ref[j, k * SHARE:(k + 1) * SHARE, :].astype(F32)
+            w_ref[j * SHARE:(j + 1) * SHARE, k * LANES:(k + 1) * LANES] = part
+    g_ref[...] = gain_of(whole_ref[0, 256:, :].astype(F32))
 
 
 def rows_kernel(x_ref, inv_ref, back_ref, out_ref):
@@ -252,6 +246,7 @@
             pltpu.VMEM((ROWS, KVW), BF16), pltpu.SemaphoreType.DMA((3,)),
         ],
     )
+    slices, value_weight, gain = lax.optimization_barrier((slices, value_weight, gain))
     columns = exchange(slices, "y")
     other_weight = lax.ppermute(value_weight, "core", SWAP)
     other_gain = lax.ppermute(gain, "core", SWAP)
@@ -264,32 +259,24 @@
 
     back, blocks = call(
         products_kernel, 1,
-        [((CHIPS, ROWS, width + LANES), F32), ((2, SHARES, SHARE, WIDE), BF16)],
+        [((CHIPS, ROWS, width + LANES), F32), ((2, SHARES, TALL, LANES), BF16)],
         core.reshape(1), columns, most, weights, gain, other_gain,
         spaces=[pltpu.VMEM] * 2 + [pltpu.HBM] + [pltpu.VMEM] * 2, out_space=pltpu.HBM, limit=52,
         flops=4 * CHIPS * ROWS * width * KVW,
         scratch=[
             pltpu.VMEM((2, OWN, KVW), BF16), pltpu.VMEM((CHIPS * ROWS, KVW), BF16),
-            pltpu.VMEM((CHIPS, ROWS, width + LANES), F32), pltpu.VMEM((2, SHARES, SHARE, WIDE), BF16),
+            pltpu.VMEM((CHIPS, ROWS, width + LANES), F32), pltpu.VMEM((2, SHARES, TALL, LANES), BF16),
             pltpu.SemaphoreType.DMA((2,)), pltpu.SemaphoreType.DMA((3,)),
         ],
     )
-    blocks = exchange(blocks.reshape(2 * SHARES, SHARE, WIDE), ("core", *PLANE))
-    (part,) = call(partial_kernel, 0, [((SHARE, WIDE), F32)], blocks)
+    blocks = exchange(blocks.reshape(2 * SHARES, TALL, LANES), ("core", *PLANE))
+    (part,) = call(partial_kernel, 0, [((TALL, LANES), F32)], blocks)
 
     part, back = lax.optimization_barrier((part.astype(jnp.float16), back.astype(jnp.float16)))
     back = exchange(back, "y")
-    theirs = lax.ppermute(part, PAIR, SWAP)
-    (part,) = call(pair_kernel, 0, [((SHARE, WIDE), F32)], part.astype(F32), theirs.astype(F32))
-    part = lax.optimization_barrier(part.astype(jnp.float16))
-    parts = [part] + [
-        lax.ppermute(part, DEEP, [(i, (i + k) % DEPTH) for i in range(DEPTH)])
-        for k in range(1, DEPTH)
-    ]
+    parts = lax.all_gather(part, DEEP, axis=0)
     (whole,) = call(
-        total_kernel, 1, [((SHARES, SHARE, WIDE), BF16)],
-        lax.axis_index(DEEP).reshape(1), *[part.astype(F32) for part in parts],
-        scratch=[pltpu.VMEM((DEPTH, SHARE, WIDE), F32)],
+        total_kernel, 0, [((SHARES, TALL, LANES), BF16)], parts.astype(F32)
     )
     whole, back = lax.optimization_barrier((whole, back))
     whole = exchange(whole, PLANE)

time: 131 us -> 128 us (0.977)
  blocking collectives: 27.4 us -> 57.3 us
  starting transfers between devices: 52.9 us -> 33.6 us
  waiting for transfers between devices: 36.9 us -> 23.1 us
    all_gather x0 -> x1, blocking collectives: none -> 30 us  [body(): parts = lax.all_gather(part, DEEP, axis=0)]
    ppermute x3 -> x0, starting transfers between devices: 20.1 us -> none  [the longest x2 14 us: body(): lax.ppermute(part, DEEP, [(i, (i + k) % DEPTH) for i in range(DEPTH)])]
    ppermute x3 -> x0, waiting for transfers between devices: 13 us -> none  [the longest x2 9.49 us: body(): lax.ppermute(part, DEEP, [(i, (i + k) % DEPTH) for i in range(DEPTH)])]
    pallas_call x8 -> x7, Pallas kernels: 10 us -> 9.84 us  [call(): pl.pallas_call(kernel, out_shape=shapes, in_specs=[SMEM] * n_scalars + ([...]
  transfers between devices with their start and end apart: 9 -> 6, of which waited for: 5 -> 2; matrix products, arithmetic and copies ran while one was open for 1% -> 1% of each run, Pallas kernels for 2% -> 2%
where the time goes in v3:
time: 128 us; the launch traced here: 127 us
  blocking collectives  57.3 us (45%)
  starting transfers between devices  33.6 us (26%)
  waiting for transfers between devices  23.1 us (18%)
  Pallas kernels  9.84 us (8%)
  local copies, waits for them, and re-layouts  1.66 us (1%)
    all_gather x1, blocking collectives, body(): parts = lax.all_gather(part, DEEP, axis=0)  30 us
    all_to_all x4, starting transfers between devices, exchange(): return lax.all_to_all(blocks, axis, 0, 0, tiled=True)  29.2 us
    all_gather x1, blocking collectives, body(): most = lax.all_gather(grads[:, :KVW - 1], 'y', axis=0, tiled=True)  27.4 us
    all_to_all x4, waiting for transfers between devices, exchange(): return lax.all_to_all(blocks, axis, 0, 0, tiled=True)  23.1 us
    pallas_call x7, Pallas kernels, call(): pl.pallas_call(kernel, out_shape=shapes, in_specs=[SMEM] * n_scalars + ([...  9.84 us
  transfers between devices with their start and end apart: 6, of which 2 were waited for; matrix products, arithmetic and copies ran while one was open for 1% of the time, Pallas kernels for 2%

profile of v3, /device:TPU:8, one launch (start us, length us, event | category | flops | bytes accessed | tf_op | source)
XLA Modules:
  0.0 127.4 jit_solution(15853050336646677665)
XLA Ops:
  0.7 2.2 %shard_map.76 = (bf16[8,64,640]{2,1,0:T(8,128)(2,1)}, f32[64,128]{1,0:T(8,128)}) custom-call(s32[1]{0:T(128)} %bitcast.1.first_ref, s32[1,512]{1,0:T(1,128)} %places_in.1, bf16[64,4096]{1,0:T(8,128)(2,1)} %bitcast.11, bf16[64,1024]{1,0:T(8,128)(2,1)} %bitcast.17), custom_call_target="tpu_custom_call" | custom-call | bytes 1345540 | tf_op jit(solution)/shard_map/pallas_call | solution.py:34
  2.9 12.9 %all-to-all-start = ((bf16[8,64,640]{2,1,0:T(8,128)(2,1)}), bf16[8,64,640]{2,1,0:T(8,128)(2,1)S(1)}, u32[]{:S(2)}, u32[]{:S(2)}) async-start(bf16[8,64,640]{2,1,0:T(8,128)(2,1)} %get-tuple-element.20), calls=%async_computation | async-start | bytes 1310720 | tf_op jit(solution)/shard_map/all_to_all | solution.py:50
  15.8 2.0 %collective-permute-start = (bf16[256,1024]{1,0:T(8,128)(2,1)S(1)}, bf16[256,1024]{1,0:T(8,128)(2,1)S(1)}, u32[]{:S(2)}, u32[]{:S(2)}) collective-permute-start(bf16[256,1024]{1,0:T(8,128)(2,1)S(1)} %copy-done.2), channel_id=1, source_target_pairs={{0,48},{48,0},{1,49},{49,1},{2,50},{50,2},{3,51},{51,3},{4,52},{52... | collective-permute-start | bytes 1572872 | tf_op jit(solution)/shard_map/ppermute | solution.py:251
  17.9 2.4 %collective-permute-start.1 = (f32[1,256]{1,0:T(1,128)S(1)}, f32[1,256]{1,0:T(1,128)S(1)}, u32[]{:S(2)}, u32[]{:S(2)}) collective-permute-start(f32[1,256]{1,0:T(1,128)S(1)} %bitcast.13), channel_id=1, source_target_pairs={{0,48},{48,0},{1,49},{49,1},{2,50},{50,2},{3,51},{51,3},{4,52},{52... | collective-permute-start | bytes 3080 | tf_op jit(solution)/shard_map/ppermute | solution.py:252
  20.3 0.0 collective-permute-done.other_ref
  20.3 0.1 shard_map.77.weights_in
  20.4 1.6 %copy-done = bf16[6,256,1024]{2,1,0:T(8,128)(2,1)} copy-done((bf16[6,256,1024]{2,1,0:T(8,128)(2,1)}, bf16[6,256,1024]{2,1,0:T(8,128)(2,1)S(1)}, u32[]{:S(2)}) %copy-start) | copy-done | bytes 3145752
  22.1 27.4 %all_gather.9.most_ref = bf16[512,1023]{1,0:T(8,128)(2,1)S(1)} all-gather(bf16[64,1023]{1,0:T(8,128)(2,1)S(1)} %bitcast.18), channel_id=1, replica_groups=mesh['y'=8,'core'=2,'zh'=3,'zm'=2,'zl'=2,'x'=4] {'y'}, dimensions={0}, use_global_device_ids=true | all-gather | bytes 1178496 | tf_op jit(solution)/shard_map/all_gather | solution.py:258
  49.4 0.0 collective-permute-done.1.other_g
  49.4 0.0 all-to-all-done.columns_ref
  49.4 4.0 %shard_map.78 = (f32[8,64,640]{2,1,0:T(8,128)}, bf16[2,8,272,128]{3,2,1,0:T(8,128)(2,1)}) custom-call(s32[1]{0:T(128)} %bitcast.3.core_ref, bf16[8,64,640]{2,1,0:T(8,128)(2,1)S(1)} %all-to-all-done.columns_ref, bf16[512,1023]{1,0:T(8,128)(2,1)S(1)} %all_gather.9.most_ref, bf16[6,256,1024]{2,1,0:T(8,128)(2,1)} %copy-done, f32[1,256]{1,0:T(1,128)S(1)} %bitcast.14, ...), custom_call_target="tpu_custom_call" | custom-call | flops 1073741824 | bytes 7275524 | tf_op jit(solution)/shard_map/pallas_call | solution.py:34
  53.5 6.4 %all-to-all-start.1 = ((bf16[16,272,128]{2,1,0:T(8,128)(2,1)}), bf16[16,272,128]{2,1,0:T(8,128)(2,1)S(1)}, u32[]{:S(2)}, u32[]{:S(2)}) async-start(bf16[16,272,128]{2,1,0:T(8,128)(2,1)} %bitcast.16), calls=%async_computation.1 | async-start | bytes 2228224 | tf_op jit(solution)/shard_map/all_to_all | solution.py:50
  59.8 0.9 convert_element_type.13
  60.8 16.1 %all-to-all-done.1.blocks_ref = bf16[16,272,128]{2,1,0:T(8,128)(2,1)S(1)} async-done(((bf16[16,272,128]{2,1,0:T(8,128)(2,1)}), bf16[16,272,128]{2,1,0:T(8,128)(2,1)S(1)}, u32[]{:S(2)}, u32[]{:S(2)}) %all-to-all-start.1) | async-done | bytes 1114144 | tf_op jit(solution)/shard_map/all_to_all | solution.py:50
  76.8 0.3 shard_map.79
  77.1 5.4 %all-to-all-start.2 = ((f16[8,64,640]{2,1,0:T(8,128)(2,1)}), f16[8,64,640]{2,1,0:T(8,128)(2,1)S(1)}, u32[]{:S(2)}, u32[]{:S(2)}) async-start(f16[8,64,640]{2,1,0:T(8,128)(2,1)} %convert_element_type.13), calls=%async_computation.2 | async-start | bytes 1310720 | tf_op jit(solution)/shard_map/all_to_all | solution.py:50
  82.5 30.0 %all-gather = f16[1632,128]{1,0:T(8,128)(2,1)S(1)} all-gather(f16[272,128]{1,0:T(8,128)(2,1)S(1)} %convert_element_type.12), channel_id=2, replica_groups=mesh['y'=8,'core'=2,'zh'=3,'zm'=2,'zl'=2,'x'=4] {'zh','zm'}, dimensions={0}, use_global_device_ids=true | all-gather | bytes 487424 | tf_op jit(solution)/shard_map/all_gather | solution.py:277
  112.5 0.1 convert.parts_ref
  112.6 1.0 shard_map.80
  113.5 4.5 %all-to-all-start.3 = ((bf16[8,272,128]{2,1,0:T(8,128)(2,1)}), bf16[8,272,128]{2,1,0:T(8,128)(2,1)S(1)}, u32[]{:S(2)}, u32[]{:S(2)}) async-start(bf16[8,272,128]{2,1,0:T(8,128)(2,1)} %shard_map.80), calls=%async_computation.3 | async-start | bytes 1114112 | tf_op jit(solution)/shard_map/all_to_all | solution.py:50
  118.0 0.1 convert_element_type.15.back_ref
  118.1 1.3 shard_map.81
  119.4 7.0 %all-to-all-done.3.whole_ref = bf16[8,272,128]{2,1,0:T(8,128)(2,1)S(1)} async-done(((bf16[8,272,128]{2,1,0:T(8,128)(2,1)}), bf16[8,272,128]{2,1,0:T(8,128)(2,1)S(1)}, u32[]{:S(2)}, u32[]{:S(2)}) %all-to-all-start.3) | async-done | bytes 557088 | tf_op jit(solution)/shard_map/all_to_all | solution.py:50
  126.4 1.0 shard_map.82
  (15 shorter events, 0.0 us)
Async XLA Ops:
  0.6 17.2 %copy-start.4 = (f32[256]{0:T(256)S(1)}, f32[256]{0:T(256)}, u32[]{:S(2)}) copy-start(f32[256]{0:T(256)} %param.9) | copy-start | bytes 3076
  0.6 15.2 %copy-start.2 = (bf16[256,1024]{1,0:T(8,128)(2,1)S(1)}, bf16[256,1024]{1,0:T(8,128)(2,1)}, u32[]{:S(2)}) copy-start(bf16[256,1024]{1,0:T(8,128)(2,1)} %mine_ref) | copy-start | bytes 1572868
  2.9 46.5 %all-to-all-start = ((bf16[8,64,640]{2,1,0:T(8,128)(2,1)}), bf16[8,64,640]{2,1,0:T(8,128)(2,1)S(1)}, u32[]{:S(2)}, u32[]{:S(2)}) async-start(bf16[8,64,640]{2,1,0:T(8,128)(2,1)} %get-tuple-element.20), calls=%async_computation | async-start | bytes 1310720 | tf_op jit(solution)/shard_map/all_to_all | solution.py:50
  15.8 6.2 %copy-start.6 = (bf16[1,64,1024]{2,1,0:T(8,128)(2,1)S(1)}, bf16[1,64,1024]{2,1,0:T(8,128)(2,1)}, u32[]{:S(2)}) copy-start(bf16[1,64,1024]{2,1,0:T(8,128)(2,1)} %param.6) | copy-start | bytes 393220
  15.8 4.5 %collective-permute-start = (bf16[256,1024]{1,0:T(8,128)(2,1)S(1)}, bf16[256,1024]{1,0:T(8,128)(2,1)S(1)}, u32[]{:S(2)}, u32[]{:S(2)}) collective-permute-start(bf16[256,1024]{1,0:T(8,128)(2,1)S(1)} %copy-done.2), channel_id=1, source_target_pairs={{0,48},{48,0},{1,49},{49,1},{2,50},{50,2},{3,51},{51,3},{4,52},{52... | collective-permute-start | bytes 1572872 | tf_op jit(solution)/shard_map/ppermute | solution.py:251
  17.9 31.5 %collective-permute-start.1 = (f32[1,256]{1,0:T(1,128)S(1)}, f32[1,256]{1,0:T(1,128)S(1)}, u32[]{:S(2)}, u32[]{:S(2)}) collective-permute-start(f32[1,256]{1,0:T(1,128)S(1)} %bitcast.13), channel_id=1, source_target_pairs={{0,48},{48,0},{1,49},{49,1},{2,50},{50,2},{3,51},{51,3},{4,52},{52... | collective-permute-start | bytes 3080 | tf_op jit(solution)/shard_map/ppermute | solution.py:252
  20.4 1.6 %copy-start = (bf16[6,256,1024]{2,1,0:T(8,128)(2,1)}, bf16[6,256,1024]{2,1,0:T(8,128)(2,1)S(1)}, u32[]{:S(2)}) copy-start(bf16[6,256,1024]{2,1,0:T(8,128)(2,1)S(1)} %shard_map.77.weights_in) | copy-start | bytes 9437188
  53.4 6.4 %copy-start.5 = (f32[8,64,640]{2,1,0:T(8,128)S(1)}, f32[8,64,640]{2,1,0:T(8,128)}, u32[]{:S(2)}) copy-start(f32[8,64,640]{2,1,0:T(8,128)} %get-tuple-element.26) | copy-start | bytes 3932164
  53.5 23.4 %all-to-all-start.1 = ((bf16[16,272,128]{2,1,0:T(8,128)(2,1)}), bf16[16,272,128]{2,1,0:T(8,128)(2,1)S(1)}, u32[]{:S(2)}, u32[]{:S(2)}) async-start(bf16[16,272,128]{2,1,0:T(8,128)(2,1)} %bitcast.16), calls=%async_computation.1 | async-start | bytes 2228224 | tf_op jit(solution)/shard_map/all_to_all | solution.py:50
  77.1 36.4 %all-to-all-start.2 = ((f16[8,64,640]{2,1,0:T(8,128)(2,1)}), f16[8,64,640]{2,1,0:T(8,128)(2,1)S(1)}, u32[]{:S(2)}, u32[]{:S(2)}) async-start(f16[8,64,640]{2,1,0:T(8,128)(2,1)} %convert_element_type.13), calls=%async_computation.2 | async-start | bytes 1310720 | tf_op jit(solution)/shard_map/all_to_all | solution.py:50
  113.5 4.6 %copy-start.1 = (bf16[1,64,4096]{2,1,0:T(8,128)(2,1)S(1)}, bf16[1,64,4096]{2,1,0:T(8,128)(2,1)}, u32[]{:S(2)}) copy-start(bf16[1,64,4096]{2,1,0:T(8,128)(2,1)} %param.5) | copy-start | bytes 1572868
  113.5 4.6 %copy-start.3 = (f32[64,128]{1,0:T(8,128)S(1)}, f32[64,128]{1,0:T(8,128)}, u32[]{:S(2)}) copy-start(f32[64,128]{1,0:T(8,128)} %get-tuple-element.18.inv_ref) | copy-start | bytes 98308
  113.5 12.9 %all-to-all-start.3 = ((bf16[8,272,128]{2,1,0:T(8,128)(2,1)}), bf16[8,272,128]{2,1,0:T(8,128)(2,1)S(1)}, u32[]{:S(2)}, u32[]{:S(2)}) async-start(bf16[8,272,128]{2,1,0:T(8,128)(2,1)} %shard_map.80), calls=%async_computation.3 | async-start | bytes 1114112 | tf_op jit(solution)/shard_map/all_to_all | solution.py:50

commit v4 on v3

--- a/solution.py
+++ b/solution.py
@@ -16,11 +16,12 @@
 OWN = D // CHIPS // 2
 SHARES = 8
 SHARE = OWN // SHARES
-DEPTH = 6
-STACK = 6
+DEPTH = 3
+STACK = 16
 TALL = 256 + 16
 PLANE = ("zl", "x")
-DEEP = ("zh", "zm")
+PAIR = "zm"
+DEEP = "zh"
 SWAP = ((0, 1), (1, 0))
 F32 = jnp.float32
 BF16 = jnp.bfloat16
@@ -111,16 +112,7 @@
     return jnp.concatenate([extra[0:1] + extra[2:3], extra[1:2] + extra[3:4]], axis=1)
 
 
-def products_kernel(
-    core_ref, columns_ref, most_ref, weights_in, mine_g, other_g, back_out, blocks_out,
-    weights_ref, dv_ref, back_ref, blocks_ref, arrived, left,
-):
-    copies = [
-        pltpu.make_async_copy(weights_in.at[i], weights_ref.at[i], arrived.at[i]) for i in range(2)
-    ]
-    for copy in copies:
-        copy.start()
-    core = core_ref[0]
+def half_products(columns_ref, most_ref, dv_ref, weight_ref, copy, gain, at, blocks_ref):
     width = D // CHIPS
     tail = KVW - LANES
     dv_ref[:, :tail] = most_ref[:, :tail]
@@ -131,37 +123,56 @@
     ending = jnp.where(lane == LANES - 1, extra[:, 0:1], dv_ref[:, tail:].astype(F32))
     dv_ref[:, tail:] = ending.astype(BF16)
     dv = dv_ref[...]
-    gained, largest, leaving = [], 0.0, []
-    for i, (half, g_ref) in enumerate(((1 - core, other_g), (core, mine_g))):
-        copies[i].wait()
-        gain = g_ref[...]
-        dnormed = lax.dot_general(dv, weights_ref[i], (((1,), (1,)), ((), ())), preferred_element_type=F32)
-        gained.append((pl.multiple_of(half * OWN, OWN), dnormed * gain))
-        largest = jnp.maximum(largest, jnp.max(jnp.abs(gained[-1][1]), axis=1, keepdims=True))
-        at = gained[-1][0]
-        normed = columns_ref[:, :, pl.ds(at, OWN)].reshape(CHIPS * ROWS, OWN).astype(F32) * inv
-        scaled = (normed * gain).astype(BF16)
-        weight = lax.dot_general(scaled, dv, (((0,), (0,)), ((), ())), preferred_element_type=F32)
-        total = jnp.sum(dnormed * normed, axis=0, keepdims=True)
-        high = rounded(total)
-        mark = gain_rows(high, total - high).astype(BF16)
-        for j in range(SHARES):
-            rows = weight[j * SHARE:(j + 1) * SHARE].astype(BF16)
-            for k in range(KVW // LANES):
-                blocks_ref[i, j, k * SHARE:(k + 1) * SHARE, :] = rows[:, k * LANES:(k + 1) * LANES]
-            blocks_ref[i, j, 256:, :] = mark
-        leaving.append(pltpu.make_async_copy(blocks_ref.at[i], blocks_out.at[half], left.at[i]))
-        leaving[-1].start()
+    normed = columns_ref[:, :, pl.ds(at, OWN)].reshape(CHIPS * ROWS, OWN).astype(F32) * inv
+    scaled = (normed * gain).astype(BF16)
+    weight = lax.dot_general(scaled, dv, (((0,), (0,)), ((), ())), preferred_element_type=F32)
+    copy.wait()
+    dnormed = lax.dot_general(dv, weight_ref[...], (((1,), (1,)), ((), ())), preferred_element_type=F32)
+    total = jnp.sum(dnormed * normed, axis=0, keepdims=True)
+    zeros = jnp.zeros((1, OWN), F32)
+    mark = gain_rows(total, zeros)
+    for j in range(SHARES):
+        rows = weight[j * SHARE:(j + 1) * SHARE]
+        for k in range(KVW // LANES):
+            blocks_ref[j, k * SHARE:(k + 1) * SHARE, :] = rows[:, k * LANES:(k + 1) * LANES]
+        blocks_ref[j, 256:, :] = mark
+    return dnormed * gain
+
+
+def theirs_kernel(core_ref, columns_ref, most_ref, weights_in, gain_ref, gained_ref, blocks_ref, weight_ref, dv_ref, arrived):
+    copy = pltpu.make_async_copy(weights_in.at[0], weight_ref, arrived.at[0])
+    copy.start()
+    at = pl.multiple_of((1 - core_ref[0]) * OWN, OWN)
+    gained_ref[...] = half_products(columns_ref, most_ref, dv_ref, weight_ref, copy, gain_ref[...], at, blocks_ref)
+
+
+def mine_kernel(core_ref, columns_ref, most_ref, weights_in, gain_ref, gained_in, back_ref, blocks_ref, weight_ref, dv_ref, gained_ref, arrived):
+    copies = [
+        pltpu.make_async_copy(weights_in.at[1], weight_ref, arrived.at[0]),
+        pltpu.make_async_copy(gained_in, gained_ref, arrived.at[1]),
+    ]
+    for copy in copies:
+        copy.start()
+    at = pl.multiple_of(core_ref[0] * OWN, OWN)
+    mine = half_products(columns_ref, most_ref, dv_ref, weight_ref, copies[0], gain_ref[...], at, blocks_ref)
+    copies[1].wait()
+    other = gained_ref[...]
+    largest = jnp.max(jnp.maximum(jnp.abs(mine), jnp.abs(other)), axis=1, keepdims=True)
     power = jnp.floor(jnp.log2(jnp.maximum(largest, 1e-30)))
     scale = jnp.exp2(-power)
-    for at, value in gained:
-        back_ref[:, :, pl.ds(at, OWN)] = (value * scale).reshape(CHIPS, ROWS, OWN)
+    back_ref[:, :, :OWN] = (mine * scale).reshape(CHIPS, ROWS, OWN)
+    back_ref[:, :, OWN:2 * OWN] = (other * scale).reshape(CHIPS, ROWS, OWN)
     power = jnp.broadcast_to(power, (CHIPS * ROWS, LANES))
-    back_ref[:, :, width:] = power.reshape(CHIPS, ROWS, LANES)
-    leaving.append(pltpu.make_async_copy(back_ref, back_out, left.at[2]))
-    leaving[-1].start()
-    for copy in leaving:
-        copy.wait()
+    back_ref[:, :, 2 * OWN:] = power.reshape(CHIPS, ROWS, LANES)
+
+
+def blocks_kernel(keep_ref, theirs_ref, blocks_ref):
+    gain = gain_of(keep_ref[0, 256:, :]) + gain_of(theirs_ref[0, 256:, :])
+    high = rounded(gain)
+    mark = gain_rows(high, gain - high).astype(BF16)
+    for j in range(SHARES):
+        blocks_ref[j, :256, :] = (keep_ref[j, :256, :] + theirs_ref[j, :256, :]).astype(BF16)
+        blocks_ref[j, 256:, :] = mark
 
 
 def exponent(value):
@@ -185,9 +196,14 @@
 
 def partial_kernel(blocks_ref, part_ref):
     total = blocks_ref[0].astype(F32)
-    for i in range(1, 2 * SHARES):
+    for i in range(1, SHARES):
         total = total + blocks_ref[i].astype(F32)
     pack(total[:256], gain_of(total[256:]), part_ref)
+
+
+def pair_kernel(parts_ref, part_ref):
+    (weight, gain), (more_weight, more_gain) = unpack(parts_ref[0]), unpack(parts_ref[1])
+    pack(weight + more_weight, gain + more_gain, part_ref)
 
 
 def total_kernel(parts_ref, out_ref):
@@ -211,23 +227,24 @@
     g_ref[...] = gain_of(whole_ref[0, 256:, :].astype(F32))
 
 
-def rows_kernel(x_ref, inv_ref, back_ref, out_ref):
-    width = D // CHIPS
+def rows_kernel(core_ref, x_ref, inv_ref, back_ref, out_ref):
+    core = core_ref[0]
+    spots = []
+    for j in range(CHIPS):
+        scale = jnp.exp2(back_ref[j, :, 2 * OWN:2 * OWN + 1])
+        for i, half in enumerate((core, 1 - core)):
+            at = pl.multiple_of((2 * j + half) * OWN, OWN)
+            spots.append((j, slice(i * OWN, (i + 1) * OWN), pl.ds(at, OWN), scale))
     total = jnp.zeros((ROWS, LANES), F32)
-    scales = [jnp.exp2(back_ref[j, :, width:width + 1]) for j in range(CHIPS)]
-    for j, scale in enumerate(scales):
-        product = back_ref[j, :, :width] * x_ref[:, j * width:(j + 1) * width].astype(F32)
-        part = product[:, :LANES]
-        for k in range(LANES, width, LANES):
-            part = part + product[:, k:k + LANES]
-        total = total + part * scale
+    for j, lanes, at, scale in spots:
+        product = back_ref[j, :, lanes] * x_ref[:, at].astype(F32)
+        total = total + (product[:, :LANES] + product[:, LANES:]) * scale
     inv = inv_ref[:, :1]
     mean = inv * (jnp.sum(total, axis=1, keepdims=True) / D)
     shift = inv * mean
-    for j, scale in enumerate(scales):
-        at = slice(j * width, (j + 1) * width)
+    for j, lanes, at, scale in spots:
         values = x_ref[:, at].astype(F32)
-        out_ref[:, at] = (inv * (back_ref[j, :, :width] * scale - values * shift)).astype(BF16)
+        out_ref[:, at] = (inv * (back_ref[j, :, lanes] * scale - values * shift)).astype(BF16)
 
 
 def body(sel_inputs, val_grads, positions, value_weight, norm_gain):
@@ -252,36 +269,50 @@
     other_gain = lax.ppermute(gain, "core", SWAP)
     (weights,) = call(
         stack_kernel, 0, [((STACK, OWN, KVW), BF16)], other_weight, value_weight,
-        spaces=[pltpu.HBM] * 2, out_space=pltpu.HBM, scratch=[pltpu.SemaphoreType.DMA((2,))],
+        spaces=[pltpu.HBM] * 2, out_space=pltpu.HBM, scratch=[pltpu.SemaphoreType.DMA((2,))], limit=50,
     )
     grads, weights = lax.optimization_barrier((grads, weights))
     most = lax.all_gather(grads[:, :KVW - 1], "y", axis=0, tiled=True)
 
-    back, blocks = call(
-        products_kernel, 1,
-        [((CHIPS, ROWS, width + LANES), F32), ((2, SHARES, TALL, LANES), BF16)],
-        core.reshape(1), columns, most, weights, gain, other_gain,
-        spaces=[pltpu.VMEM] * 2 + [pltpu.HBM] + [pltpu.VMEM] * 2, out_space=pltpu.HBM, limit=52,
-        flops=4 * CHIPS * ROWS * width * KVW,
+    spaces = [pltpu.VMEM] * 2 + [pltpu.HBM, pltpu.VMEM]
+    shape = ((SHARES, TALL, LANES), F32)
+    gained, send = call(
+        theirs_kernel, 1, [((CHIPS * ROWS, OWN), F32), shape],
+        core.reshape(1), columns, most, weights, other_gain,
+        spaces=spaces, limit=47, flops=2 * CHIPS * ROWS * width * KVW,
         scratch=[
-            pltpu.VMEM((2, OWN, KVW), BF16), pltpu.VMEM((CHIPS * ROWS, KVW), BF16),
-            pltpu.VMEM((CHIPS, ROWS, width + LANES), F32), pltpu.VMEM((2, SHARES, TALL, LANES), BF16),
-            pltpu.SemaphoreType.DMA((2,)), pltpu.SemaphoreType.DMA((3,)),
+            pltpu.VMEM((OWN, KVW), BF16), pltpu.VMEM((CHIPS * ROWS, KVW), BF16),
+            pltpu.SemaphoreType.DMA((1,)),
         ],
     )
-    blocks = exchange(blocks.reshape(2 * SHARES, TALL, LANES), ("core", *PLANE))
+    theirs = lax.ppermute(send, "core", SWAP)
+    back, keep = call(
+        mine_kernel, 1, [((CHIPS, ROWS, width + LANES), F32), shape],
+        core.reshape(1), columns, most, weights, gain, gained,
+        spaces=spaces + [pltpu.HBM], limit=47, flops=2 * CHIPS * ROWS * width * KVW,
+        scratch=[
+            pltpu.VMEM((OWN, KVW), BF16), pltpu.VMEM((CHIPS * ROWS, KVW), BF16),
+            pltpu.VMEM((CHIPS * ROWS, OWN), F32), pltpu.SemaphoreType.DMA((2,)),
+        ],
+    )
+    (blocks,) = call(blocks_kernel, 0, [((SHARES, TALL, LANES), BF16)], keep, theirs)
+    blocks = exchange(blocks, PLANE)
     (part,) = call(partial_kernel, 0, [((TALL, LANES), F32)], blocks)
 
     part, back = lax.optimization_barrier((part.astype(jnp.float16), back.astype(jnp.float16)))
     back = exchange(back, "y")
-    parts = lax.all_gather(part, DEEP, axis=0)
+    parts = lax.all_gather(part, PAIR, axis=0)
+    (part,) = call(pair_kernel, 0, [((TALL, LANES), F32)], parts.astype(F32))
+    parts = lax.all_gather(part.astype(jnp.float16), DEEP, axis=0)
     (whole,) = call(
         total_kernel, 0, [((SHARES, TALL, LANES), BF16)], parts.astype(F32)
     )
     whole, back = lax.optimization_barrier((whole, back))
     whole = exchange(whole, PLANE)
 
-    (result,) = call(rows_kernel, 0, [((ROWS, D), BF16)], inputs, inv, back.astype(F32))
+    (result,) = call(
+        rows_kernel, 1, [((ROWS, D), BF16)], core.reshape(1), inputs, inv, back.astype(F32)
+    )
     weight_grad, gain_grad = call(
         finish_kernel, 0, [((OWN, KVW), F32), ((1, OWN), F32)], whole
     )

time: 128 us -> 123 us (0.961)
  waiting for transfers between devices: 23.1 us -> 17 us
  starting transfers between devices: 33.6 us -> 35.7 us
  Pallas kernels: 9.84 us -> 11.7 us
  local copies, waits for them, and re-layouts: 1.66 us -> 0.02 us
    all_to_all x4, waiting for transfers between devices: 23.1 us -> 16.1 us  [exchange(): return lax.all_to_all(blocks, axis, 0, 0, tiled=True)]
    ppermute x0 -> x1, starting transfers between devices: none -> 1.92 us  [body(): theirs = lax.ppermute(send, 'core', SWAP)]
    pallas_call x7 -> x10, Pallas kernels: 9.84 us -> 11.7 us  [call(): pl.pallas_call(kernel, out_shape=shapes, in_specs=[SMEM] * n_scalars + ([...]
    unnamed x14 -> x10, local copies, waits for them, and re-layouts: 1.66 us -> 0.02 us
    all_gather x1 -> x2, blocking collectives: 30 us -> 28.5 us  [the longest x1 21.4 us: body(): parts = lax.all_gather(part.astype(jnp.float16), DEEP, axis=0)]
  transfers between devices with their start and end apart: 6 -> 7, of which waited for: 2 -> 3; matrix products, arithmetic and copies ran while one was open for 1% -> 1% of each run, Pallas kernels for 2% -> 4%
where the time goes in v4:
time: 123 us; the launch traced here: 122 us
  blocking collectives  56.1 us (46%)
  starting transfers between devices  35.7 us (29%)
  waiting for transfers between devices  17 us (14%)
  Pallas kernels  11.7 us (10%)
    all_to_all x4, starting transfers between devices, exchange(): return lax.all_to_all(blocks, axis, 0, 0, tiled=True)  29.3 us
    all_gather x1, blocking collectives, body(): most = lax.all_gather(grads[:, :KVW - 1], 'y', axis=0, tiled=True)  27.5 us
    all_gather x1, blocking collectives, body(): parts = lax.all_gather(part.astype(jnp.float16), DEEP, axis=0)  21.4 us
    all_to_all x4, waiting for transfers between devices, exchange(): return lax.all_to_all(blocks, axis, 0, 0, tiled=True)  16.1 us
    pallas_call x10, Pallas kernels, call(): pl.pallas_call(kernel, out_shape=shapes, in_specs=[SMEM] * n_scalars + ([...  11.7 us
    all_gather x1, blocking collectives, body(): parts = lax.all_gather(part, PAIR, axis=0)  7.12 us
  transfers between devices with their start and end apart: 7, of which 3 were waited for; matrix products, arithmetic and copies ran while one was open for 1% of the time, Pallas kernels for 4%

profile of v4, /device:TPU:8, one launch (start us, length us, event | category | flops | bytes accessed | tf_op | source)
XLA Modules:
  0.0 122.4 jit_solution(12481627468921854240)
XLA Ops:
  0.7 2.2 %shard_map.76 = (bf16[8,64,640]{2,1,0:T(8,128)(2,1)}, f32[64,128]{1,0:T(8,128)}) custom-call(s32[1]{0:T(128)} %bitcast.2.first_ref, s32[1,512]{1,0:T(1,128)} %places_in.1, bf16[64,4096]{1,0:T(8,128)(2,1)} %bitcast.12, bf16[64,1024]{1,0:T(8,128)(2,1)} %bitcast.18), custom_call_target="tpu_custom_call" | custom-call | bytes 1345540 | tf_op jit(solution)/shard_map/pallas_call | solution.py:35
  2.9 12.9 %all-to-all-start = ((bf16[8,64,640]{2,1,0:T(8,128)(2,1)}), bf16[8,64,640]{2,1,0:T(8,128)(2,1)S(1)}, u32[]{:S(2)}, u32[]{:S(2)}) async-start(bf16[8,64,640]{2,1,0:T(8,128)(2,1)} %get-tuple-element.22), calls=%async_computation | async-start | bytes 1310720 | tf_op jit(solution)/shard_map/all_to_all | solution.py:51
  15.8 2.0 %collective-permute-start = (bf16[256,1024]{1,0:T(8,128)(2,1)S(1)}, bf16[256,1024]{1,0:T(8,128)(2,1)S(1)}, u32[]{:S(2)}, u32[]{:S(2)}) collective-permute-start(bf16[256,1024]{1,0:T(8,128)(2,1)S(1)} %copy-done.1), channel_id=1, source_target_pairs={{0,48},{48,0},{1,49},{49,1},{2,50},{50,2},{3,51},{51,3},{4,52},{52... | collective-permute-start | bytes 1572872 | tf_op jit(solution)/shard_map/ppermute | solution.py:268
  17.9 2.4 %collective-permute-start.1 = (f32[1,256]{1,0:T(1,128)S(1)}, f32[1,256]{1,0:T(1,128)S(1)}, u32[]{:S(2)}, u32[]{:S(2)}) collective-permute-start(f32[1,256]{1,0:T(1,128)S(1)} %bitcast.14), channel_id=1, source_target_pairs={{0,48},{48,0},{1,49},{49,1},{2,50},{50,2},{3,51},{51,3},{4,52},{52... | collective-permute-start | bytes 3080 | tf_op jit(solution)/shard_map/ppermute | solution.py:269
  20.3 1.0 shard_map.77.weights_in
  21.3 27.5 %all_gather.15.most_ref = bf16[512,1023]{1,0:T(8,128)(2,1)S(1)} all-gather(bf16[64,1023]{1,0:T(8,128)(2,1)S(1)} %bitcast.19), channel_id=1, replica_groups=mesh['y'=8,'core'=2,'zh'=3,'zm'=2,'zl'=2,'x'=4] {'y'}, dimensions={0}, use_global_device_ids=true | all-gather | bytes 1178496 | tf_op jit(solution)/shard_map/all_gather | solution.py:275
  48.9 2.1 %shard_map.78 = (f32[512,256]{1,0:T(8,128)S(1)}, f32[8,272,128]{2,1,0:T(8,128)S(1)}) custom-call(s32[1]{0:T(128)} %bitcast.core_ref, bf16[8,64,640]{2,1,0:T(8,128)(2,1)S(1)} %all-to-all-done.columns_ref, bf16[512,1023]{1,0:T(8,128)(2,1)S(1)} %all_gather.15.most_ref, bf16[16,256,1024]{2,1,0:T(8,128)(2,1)} %shard_map.77.weights_in, ...), custom_call_target="tpu_custom_call" | custom-call | flops 536870912 | bytes 11730948 | tf_op jit(solution)/shard_map/pallas_call | solution.py:35
  51.0 1.9 %collective-permute-start.2 = (f32[8,272,128]{2,1,0:T(8,128)S(1)}, f32[8,272,128]{2,1,0:T(8,128)S(1)}, u32[]{:S(2)}, u32[]{:S(2)}) collective-permute-start(f32[8,272,128]{2,1,0:T(8,128)S(1)} %get-tuple-element.29), channel_id=1, source_target_pairs={{0,48},{48,0},{1,49},{49,1},{2,50},{50,2},{3,51},{51,3},{4,52},{52... | collective-permute-start | bytes 3342344 | tf_op jit(solution)/shard_map/ppermute | solution.py:288
  52.9 1.8 %shard_map.79 = (f32[8,64,640]{2,1,0:T(8,128)S(1)}, f32[8,272,128]{2,1,0:T(8,128)S(1)}) custom-call(s32[1]{0:T(128)} %bitcast.core_ref, bf16[8,64,640]{2,1,0:T(8,128)(2,1)S(1)} %all-to-all-done.columns_ref, bf16[512,1023]{1,0:T(8,128)(2,1)S(1)} %all_gather.15.most_ref, bf16[16,256,1024]{2,1,0:T(8,128)(2,1)} %shard_map.77.weights_in, f32[1,256]{1,0:T(1,128)S(1)} %bitcast.15, ...), custom_call_target="tpu_custom_call" | custom-call | flops 536870912 | bytes 13041668 | tf_op jit(solution)/shard_map/pallas_call | solution.py:35
  54.7 0.9 collective-permute-done.2.theirs_ref
  55.6 0.9 shard_map.80
  56.5 6.7 %all-to-all-start.1 = ((bf16[8,272,128]{2,1,0:T(8,128)(2,1)}), bf16[8,272,128]{2,1,0:T(8,128)(2,1)S(1)}, u32[]{:S(2)}, u32[]{:S(2)}) async-start(bf16[8,272,128]{2,1,0:T(8,128)(2,1)} %shard_map.80), calls=%async_computation.1 | async-start | bytes 1114112 | tf_op jit(solution)/shard_map/all_to_all | solution.py:51
  63.3 0.9 convert_element_type.19
  64.2 9.1 %all-to-all-done.1.blocks_ref = bf16[8,272,128]{2,1,0:T(8,128)(2,1)S(1)} async-done(((bf16[8,272,128]{2,1,0:T(8,128)(2,1)}), bf16[8,272,128]{2,1,0:T(8,128)(2,1)S(1)}, u32[]{:S(2)}, u32[]{:S(2)}) %all-to-all-start.1) | async-done | bytes 557088 | tf_op jit(solution)/shard_map/all_to_all | solution.py:51
  73.3 0.2 shard_map.81
  73.5 5.4 %all-to-all-start.2 = ((f16[8,64,640]{2,1,0:T(8,128)(2,1)}), f16[8,64,640]{2,1,0:T(8,128)(2,1)S(1)}, u32[]{:S(2)}, u32[]{:S(2)}) async-start(f16[8,64,640]{2,1,0:T(8,128)(2,1)} %convert_element_type.19), calls=%async_computation.2 | async-start | bytes 1310720 | tf_op jit(solution)/shard_map/all_to_all | solution.py:51
  78.9 7.1 %all-gather = f16[544,128]{1,0:T(8,128)(2,1)S(1)} all-gather(f16[272,128]{1,0:T(8,128)(2,1)S(1)} %convert_element_type.18), channel_id=2, replica_groups=mesh['y'=8,'core'=2,'zh'=3,'zm'=2,'zl'=2,'x'=4] {'zm'}, dimensions={0}, use_global_device_ids=true | all-gather | bytes 208896 | tf_op jit(solution)/shard_map/all_gather | solution.py:304
  86.1 0.2 shard_map.82
  86.3 21.4 %all-gather.1 = f16[816,128]{1,0:T(8,128)(2,1)S(1)} all-gather(f16[272,128]{1,0:T(8,128)(2,1)S(1)} %convert_element_type.21), channel_id=3, replica_groups=mesh['y'=8,'core'=2,'zh'=3,'zm'=2,'zl'=2,'x'=4] {'zh'}, dimensions={0}, use_global_device_ids=true | all-gather | bytes 278528 | tf_op jit(solution)/shard_map/all_gather | solution.py:306
  107.7 0.9 shard_map.83
  108.7 4.3 %all-to-all-start.3 = ((bf16[8,272,128]{2,1,0:T(8,128)(2,1)}), bf16[8,272,128]{2,1,0:T(8,128)(2,1)S(1)}, u32[]{:S(2)}, u32[]{:S(2)}) async-start(bf16[8,272,128]{2,1,0:T(8,128)(2,1)} %shard_map.83), calls=%async_computation.3 | async-start | bytes 1114112 | tf_op jit(solution)/shard_map/all_to_all | solution.py:51
  113.1 1.3 %shard_map.84 = bf16[64,4096]{1,0:T(8,128)(2,1)} custom-call(s32[1]{0:T(128)} %bitcast.core_ref, bf16[64,4096]{1,0:T(8,128)(2,1)S(1)} %bitcast.13, f32[64,128]{1,0:T(8,128)S(1)} %copy-done.2, f32[8,64,640]{2,1,0:T(8,128)S(1)} %convert_element_type.23.back_ref), custom_call_target="tpu_custom_call" | custom-call | bytes 2392068 | tf_op jit(solution)/shard_map/pallas_call | solution.py:35
  114.4 7.0 %all-to-all-done.3.whole_ref = bf16[8,272,128]{2,1,0:T(8,128)(2,1)S(1)} async-done(((bf16[8,272,128]{2,1,0:T(8,128)(2,1)}), bf16[8,272,128]{2,1,0:T(8,128)(2,1)S(1)}, u32[]{:S(2)}, u32[]{:S(2)}) %all-to-all-start.3) | async-done | bytes 557088 | tf_op jit(solution)/shard_map/all_to_all | solution.py:51
  121.4 1.0 shard_map.85
  (19 shorter events, 0.2 us)
Async XLA Ops:
  0.6 17.2 %copy-start.3 = (f32[256]{0:T(256)S(1)}, f32[256]{0:T(256)}, u32[]{:S(2)}) copy-start(f32[256]{0:T(256)} %param.9) | copy-start | bytes 3076
  0.6 15.2 %copy-start.1 = (bf16[256,1024]{1,0:T(8,128)(2,1)S(1)}, bf16[256,1024]{1,0:T(8,128)(2,1)}, u32[]{:S(2)}) copy-start(bf16[256,1024]{1,0:T(8,128)(2,1)} %mine_ref) | copy-start | bytes 1572868
  2.9 46.0 %all-to-all-start = ((bf16[8,64,640]{2,1,0:T(8,128)(2,1)}), bf16[8,64,640]{2,1,0:T(8,128)(2,1)S(1)}, u32[]{:S(2)}, u32[]{:S(2)}) async-start(bf16[8,64,640]{2,1,0:T(8,128)(2,1)} %get-tuple-element.22), calls=%async_computation | async-start | bytes 1310720 | tf_op jit(solution)/shard_map/all_to_all | solution.py:51
  15.8 5.5 %copy-start.4 = (bf16[1,64,1024]{2,1,0:T(8,128)(2,1)S(1)}, bf16[1,64,1024]{2,1,0:T(8,128)(2,1)}, u32[]{:S(2)}) copy-start(bf16[1,64,1024]{2,1,0:T(8,128)(2,1)} %param.6) | copy-start | bytes 393220
  15.8 4.5 %collective-permute-start = (bf16[256,1024]{1,0:T(8,128)(2,1)S(1)}, bf16[256,1024]{1,0:T(8,128)(2,1)S(1)}, u32[]{:S(2)}, u32[]{:S(2)}) collective-permute-start(bf16[256,1024]{1,0:T(8,128)(2,1)S(1)} %copy-done.1), channel_id=1, source_target_pairs={{0,48},{48,0},{1,49},{49,1},{2,50},{50,2},{3,51},{51,3},{4,52},{52... | collective-permute-start | bytes 1572872 | tf_op jit(solution)/shard_map/ppermute | solution.py:268
  17.9 31.0 %collective-permute-start.1 = (f32[1,256]{1,0:T(1,128)S(1)}, f32[1,256]{1,0:T(1,128)S(1)}, u32[]{:S(2)}, u32[]{:S(2)}) collective-permute-start(f32[1,256]{1,0:T(1,128)S(1)} %bitcast.14), channel_id=1, source_target_pairs={{0,48},{48,0},{1,49},{49,1},{2,50},{50,2},{3,51},{51,3},{4,52},{52... | collective-permute-start | bytes 3080 | tf_op jit(solution)/shard_map/ppermute | solution.py:269
  51.0 4.6 %collective-permute-start.2 = (f32[8,272,128]{2,1,0:T(8,128)S(1)}, f32[8,272,128]{2,1,0:T(8,128)S(1)}, u32[]{:S(2)}, u32[]{:S(2)}) collective-permute-start(f32[8,272,128]{2,1,0:T(8,128)S(1)} %get-tuple-element.29), channel_id=1, source_target_pairs={{0,48},{48,0},{1,49},{49,1},{2,50},{50,2},{3,51},{51,3},{4,52},{52... | collective-permute-start | bytes 3342344 | tf_op jit(solution)/shard_map/ppermute | solution.py:288
  56.5 16.7 %all-to-all-start.1 = ((bf16[8,272,128]{2,1,0:T(8,128)(2,1)}), bf16[8,272,128]{2,1,0:T(8,128)(2,1)S(1)}, u32[]{:S(2)}, u32[]{:S(2)}) async-start(bf16[8,272,128]{2,1,0:T(8,128)(2,1)} %shard_map.80), calls=%async_computation.1 | async-start | bytes 1114112 | tf_op jit(solution)/shard_map/all_to_all | solution.py:51
  73.5 35.2 %all-to-all-start.2 = ((f16[8,64,640]{2,1,0:T(8,128)(2,1)}), f16[8,64,640]{2,1,0:T(8,128)(2,1)S(1)}, u32[]{:S(2)}, u32[]{:S(2)}) async-start(f16[8,64,640]{2,1,0:T(8,128)(2,1)} %convert_element_type.19), calls=%async_computation.2 | async-start | bytes 1310720 | tf_op jit(solution)/shard_map/all_to_all | solution.py:51
  108.6 4.4 %copy-start = (bf16[1,64,4096]{2,1,0:T(8,128)(2,1)S(1)}, bf16[1,64,4096]{2,1,0:T(8,128)(2,1)}, u32[]{:S(2)}) copy-start(bf16[1,64,4096]{2,1,0:T(8,128)(2,1)} %param.5) | copy-start | bytes 1572868
  108.7 4.4 %copy-start.2 = (f32[64,128]{1,0:T(8,128)S(1)}, f32[64,128]{1,0:T(8,128)}, u32[]{:S(2)}) copy-start(f32[64,128]{1,0:T(8,128)} %get-tuple-element.20.inv_ref) | copy-start | bytes 98308
  108.7 12.7 %all-to-all-start.3 = ((bf16[8,272,128]{2,1,0:T(8,128)(2,1)}), bf16[8,272,128]{2,1,0:T(8,128)(2,1)S(1)}, u32[]{:S(2)}, u32[]{:S(2)}) async-start(bf16[8,272,128]{2,1,0:T(8,128)(2,1)} %shard_map.83), calls=%async_computation.3 | async-start | bytes 1114112 | tf_op jit(solution)/shard_map/all_to_all | solution.py:51

commit v5 on v4

--- a/solution.py
+++ b/solution.py
@@ -51,16 +51,7 @@
     return lax.all_to_all(blocks, axis, 0, 0, tiled=True)
 
 
-def prepare_kernel(first_ref, places_in, x_in, dv_in, slices_ref, inv_ref, places_ref, x_ref, dv_ref, arrived):
-    copies = [
-        pltpu.make_async_copy(x_in, x_ref, arrived.at[0]),
-        pltpu.make_async_copy(dv_in, dv_ref, arrived.at[1]),
-        pltpu.make_async_copy(places_in, places_ref, arrived.at[2]),
-    ]
-    for copy in copies:
-        copy.start()
-    for copy in copies:
-        copy.wait()
+def prepare_kernel(first_ref, places_ref, x_ref, dv_ref, slices_ref, inv_ref):
     first = first_ref[0]
     places = places_ref[...]
     inside = jnp.where((places >= first) & (places < first + TOK_DEV), 1.0, 0.0)
@@ -257,11 +248,7 @@
         prepare_kernel, 1,
         [((CHIPS, ROWS, width + LANES), BF16), ((ROWS, LANES), F32)],
         first, positions, inputs, grads,
-        spaces=[pltpu.HBM] * 3, limit=56,
-        scratch=[
-            pltpu.VMEM(positions.shape, jnp.int32), pltpu.VMEM((ROWS, D), BF16),
-            pltpu.VMEM((ROWS, KVW), BF16), pltpu.SemaphoreType.DMA((3,)),
-        ],
+        limit=56,
     )
     slices, value_weight, gain = lax.optimization_barrier((slices, value_weight, gain))
     columns = exchange(slices, "y")

time: 123 us -> 123 us (level)
  no operation moved by 1% of the time
where the time goes in v5:
time: 123 us; the launch traced here: 122 us
  blocking collectives  56 us (46%)
  starting transfers between devices  35.7 us (29%)
  waiting for transfers between devices  17 us (14%)
  Pallas kernels  11.7 us (10%)
    all_to_all x4, starting transfers between devices, exchange(): return lax.all_to_all(blocks, axis, 0, 0, tiled=True)  29.4 us
    all_gather x1, blocking collectives, body(): most = lax.all_gather(grads[:, :KVW - 1], 'y', axis=0, tiled=True)  27.5 us
    all_gather x1, blocking collectives, body(): parts = lax.all_gather(part.astype(jnp.float16), DEEP, axis=0)  21.4 us
    all_to_all x4, waiting for transfers between devices, exchange(): return lax.all_to_all(blocks, axis, 0, 0, tiled=True)  16.1 us
    pallas_call x10, Pallas kernels, call(): pl.pallas_call(kernel, out_shape=shapes, in_specs=[SMEM] * n_scalars + ([...  11.7 us
    all_gather x1, blocking collectives, body(): parts = lax.all_gather(part, PAIR, axis=0)  7.12 us
  transfers between devices with their start and end apart: 7, of which 3 were waited for; matrix products, arithmetic and copies ran while one was open for 1% of the time, Pallas kernels for 4%

profile of v5, /device:TPU:8, one launch (start us, length us, event | category | flops | bytes accessed | tf_op | source)
XLA Modules:
  0.0 122.4 jit_solution(16701499898182700214)
XLA Ops:
  0.7 2.2 %shard_map.76 = (bf16[8,64,640]{2,1,0:T(8,128)(2,1)}, f32[64,128]{1,0:T(8,128)}) custom-call(s32[1]{0:T(128)} %bitcast.2.first_ref, s32[1,512]{1,0:T(1,128)} %places_ref.1, bf16[64,4096]{1,0:T(8,128)(2,1)} %bitcast.12, bf16[64,1024]{1,0:T(8,128)(2,1)} %bitcast.18), custom_call_target="tpu_custom_call" | custom-call | bytes 1345540 | tf_op jit(solution)/shard_map/pallas_call | solution.py:35
  2.9 12.9 %all-to-all-start = ((bf16[8,64,640]{2,1,0:T(8,128)(2,1)}), bf16[8,64,640]{2,1,0:T(8,128)(2,1)S(1)}, u32[]{:S(2)}, u32[]{:S(2)}) async-start(bf16[8,64,640]{2,1,0:T(8,128)(2,1)} %get-tuple-element.22), calls=%async_computation | async-start | bytes 1310720 | tf_op jit(solution)/shard_map/all_to_all | solution.py:51
  15.8 2.0 %collective-permute-start = (bf16[256,1024]{1,0:T(8,128)(2,1)S(1)}, bf16[256,1024]{1,0:T(8,128)(2,1)S(1)}, u32[]{:S(2)}, u32[]{:S(2)}) collective-permute-start(bf16[256,1024]{1,0:T(8,128)(2,1)S(1)} %copy-done.1), channel_id=1, source_target_pairs={{0,48},{48,0},{1,49},{49,1},{2,50},{50,2},{3,51},{51,3},{4,52},{52... | collective-permute-start | bytes 1572872 | tf_op jit(solution)/shard_map/ppermute | solution.py:255
  17.9 2.4 %collective-permute-start.1 = (f32[1,256]{1,0:T(1,128)S(1)}, f32[1,256]{1,0:T(1,128)S(1)}, u32[]{:S(2)}, u32[]{:S(2)}) collective-permute-start(f32[1,256]{1,0:T(1,128)S(1)} %bitcast.14), channel_id=1, source_target_pairs={{0,48},{48,0},{1,49},{49,1},{2,50},{50,2},{3,51},{51,3},{4,52},{52... | collective-permute-start | bytes 3080 | tf_op jit(solution)/shard_map/ppermute | solution.py:256
  20.3 1.0 shard_map.77.weights_in
  21.3 27.5 %all_gather.15.most_ref = bf16[512,1023]{1,0:T(8,128)(2,1)S(1)} all-gather(bf16[64,1023]{1,0:T(8,128)(2,1)S(1)} %bitcast.19), channel_id=1, replica_groups=mesh['y'=8,'core'=2,'zh'=3,'zm'=2,'zl'=2,'x'=4] {'y'}, dimensions={0}, use_global_device_ids=true | all-gather | bytes 1178496 | tf_op jit(solution)/shard_map/all_gather | solution.py:262
  48.8 2.1 %shard_map.78 = (f32[512,256]{1,0:T(8,128)S(1)}, f32[8,272,128]{2,1,0:T(8,128)S(1)}) custom-call(s32[1]{0:T(128)} %bitcast.core_ref, bf16[8,64,640]{2,1,0:T(8,128)(2,1)S(1)} %all-to-all-done.columns_ref, bf16[512,1023]{1,0:T(8,128)(2,1)S(1)} %all_gather.15.most_ref, bf16[16,256,1024]{2,1,0:T(8,128)(2,1)} %shard_map.77.weights_in, ...), custom_call_target="tpu_custom_call" | custom-call | flops 536870912 | bytes 11730948 | tf_op jit(solution)/shard_map/pallas_call | solution.py:35
  51.0 1.9 %collective-permute-start.2 = (f32[8,272,128]{2,1,0:T(8,128)S(1)}, f32[8,272,128]{2,1,0:T(8,128)S(1)}, u32[]{:S(2)}, u32[]{:S(2)}) collective-permute-start(f32[8,272,128]{2,1,0:T(8,128)S(1)} %get-tuple-element.29), channel_id=1, source_target_pairs={{0,48},{48,0},{1,49},{49,1},{2,50},{50,2},{3,51},{51,3},{4,52},{52... | collective-permute-start | bytes 3342344 | tf_op jit(solution)/shard_map/ppermute | solution.py:275
  52.9 1.8 %shard_map.79 = (f32[8,64,640]{2,1,0:T(8,128)S(1)}, f32[8,272,128]{2,1,0:T(8,128)S(1)}) custom-call(s32[1]{0:T(128)} %bitcast.core_ref, bf16[8,64,640]{2,1,0:T(8,128)(2,1)S(1)} %all-to-all-done.columns_ref, bf16[512,1023]{1,0:T(8,128)(2,1)S(1)} %all_gather.15.most_ref, bf16[16,256,1024]{2,1,0:T(8,128)(2,1)} %shard_map.77.weights_in, f32[1,256]{1,0:T(1,128)S(1)} %bitcast.15, ...), custom_call_target="tpu_custom_call" | custom-call | flops 536870912 | bytes 13041668 | tf_op jit(solution)/shard_map/pallas_call | solution.py:35
  54.7 0.9 collective-permute-done.2.theirs_ref
  55.6 0.9 shard_map.80
  56.5 6.7 %all-to-all-start.1 = ((bf16[8,272,128]{2,1,0:T(8,128)(2,1)}), bf16[8,272,128]{2,1,0:T(8,128)(2,1)S(1)}, u32[]{:S(2)}, u32[]{:S(2)}) async-start(bf16[8,272,128]{2,1,0:T(8,128)(2,1)} %shard_map.80), calls=%async_computation.1 | async-start | bytes 1114112 | tf_op jit(solution)/shard_map/all_to_all | solution.py:51
  63.2 0.9 convert_element_type.19
  64.1 9.1 %all-to-all-done.1.blocks_ref = bf16[8,272,128]{2,1,0:T(8,128)(2,1)S(1)} async-done(((bf16[8,272,128]{2,1,0:T(8,128)(2,1)}), bf16[8,272,128]{2,1,0:T(8,128)(2,1)S(1)}, u32[]{:S(2)}, u32[]{:S(2)}) %all-to-all-start.1) | async-done | bytes 557088 | tf_op jit(solution)/shard_map/all_to_all | solution.py:51
  73.3 0.2 shard_map.81
  73.5 5.4 %all-to-all-start.2 = ((f16[8,64,640]{2,1,0:T(8,128)(2,1)}), f16[8,64,640]{2,1,0:T(8,128)(2,1)S(1)}, u32[]{:S(2)}, u32[]{:S(2)}) async-start(f16[8,64,640]{2,1,0:T(8,128)(2,1)} %convert_element_type.19), calls=%async_computation.2 | async-start | bytes 1310720 | tf_op jit(solution)/shard_map/all_to_all | solution.py:51
  78.9 7.1 %all-gather = f16[544,128]{1,0:T(8,128)(2,1)S(1)} all-gather(f16[272,128]{1,0:T(8,128)(2,1)S(1)} %convert_element_type.18), channel_id=2, replica_groups=mesh['y'=8,'core'=2,'zh'=3,'zm'=2,'zl'=2,'x'=4] {'zm'}, dimensions={0}, use_global_device_ids=true | all-gather | bytes 208896 | tf_op jit(solution)/shard_map/all_gather | solution.py:291
  86.0 0.2 shard_map.82
  86.2 21.4 %all-gather.1 = f16[816,128]{1,0:T(8,128)(2,1)S(1)} all-gather(f16[272,128]{1,0:T(8,128)(2,1)S(1)} %convert_element_type.21), channel_id=3, replica_groups=mesh['y'=8,'core'=2,'zh'=3,'zm'=2,'zl'=2,'x'=4] {'zh'}, dimensions={0}, use_global_device_ids=true | all-gather | bytes 278528 | tf_op jit(solution)/shard_map/all_gather | solution.py:293
  107.7 0.9 shard_map.83
  108.6 4.3 %all-to-all-start.3 = ((bf16[8,272,128]{2,1,0:T(8,128)(2,1)}), bf16[8,272,128]{2,1,0:T(8,128)(2,1)S(1)}, u32[]{:S(2)}, u32[]{:S(2)}) async-start(bf16[8,272,128]{2,1,0:T(8,128)(2,1)} %shard_map.83), calls=%async_computation.3 | async-start | bytes 1114112 | tf_op jit(solution)/shard_map/all_to_all | solution.py:51
  113.0 1.3 %shard_map.84 = bf16[64,4096]{1,0:T(8,128)(2,1)} custom-call(s32[1]{0:T(128)} %bitcast.core_ref, bf16[64,4096]{1,0:T(8,128)(2,1)S(1)} %bitcast.13, f32[64,128]{1,0:T(8,128)S(1)} %copy-done.2, f32[8,64,640]{2,1,0:T(8,128)S(1)} %convert_element_type.23.back_ref), custom_call_target="tpu_custom_call" | custom-call | bytes 2392068 | tf_op jit(solution)/shard_map/pallas_call | solution.py:35
  114.4 7.0 %all-to-all-done.3.whole_ref = bf16[8,272,128]{2,1,0:T(8,128)(2,1)S(1)} async-done(((bf16[8,272,128]{2,1,0:T(8,128)(2,1)}), bf16[8,272,128]{2,1,0:T(8,128)(2,1)S(1)}, u32[]{:S(2)}, u32[]{:S(2)}) %all-to-all-start.3) | async-done | bytes 557088 | tf_op jit(solution)/shard_map/all_to_all | solution.py:51
  121.3 1.0 shard_map.85
  (19 shorter events, 0.2 us)
Async XLA Ops:
  0.6 17.2 %copy-start.3 = (f32[256]{0:T(256)S(1)}, f32[256]{0:T(256)}, u32[]{:S(2)}) copy-start(f32[256]{0:T(256)} %param.9) | copy-start | bytes 3076
  0.6 15.2 %copy-start.1 = (bf16[256,1024]{1,0:T(8,128)(2,1)S(1)}, bf16[256,1024]{1,0:T(8,128)(2,1)}, u32[]{:S(2)}) copy-start(bf16[256,1024]{1,0:T(8,128)(2,1)} %mine_ref) | copy-start | bytes 1572868
  2.9 45.9 %all-to-all-start = ((bf16[8,64,640]{2,1,0:T(8,128)(2,1)}), bf16[8,64,640]{2,1,0:T(8,128)(2,1)S(1)}, u32[]{:S(2)}, u32[]{:S(2)}) async-start(bf16[8,64,640]{2,1,0:T(8,128)(2,1)} %get-tuple-element.22), calls=%async_computation | async-start | bytes 1310720 | tf_op jit(solution)/shard_map/all_to_all | solution.py:51
  15.8 5.5 %copy-start.4 = (bf16[1,64,1024]{2,1,0:T(8,128)(2,1)S(1)}, bf16[1,64,1024]{2,1,0:T(8,128)(2,1)}, u32[]{:S(2)}) copy-start(bf16[1,64,1024]{2,1,0:T(8,128)(2,1)} %param.6) | copy-start | bytes 393220
  15.8 4.5 %collective-permute-start = (bf16[256,1024]{1,0:T(8,128)(2,1)S(1)}, bf16[256,1024]{1,0:T(8,128)(2,1)S(1)}, u32[]{:S(2)}, u32[]{:S(2)}) collective-permute-start(bf16[256,1024]{1,0:T(8,128)(2,1)S(1)} %copy-done.1), channel_id=1, source_target_pairs={{0,48},{48,0},{1,49},{49,1},{2,50},{50,2},{3,51},{51,3},{4,52},{52... | collective-permute-start | bytes 1572872 | tf_op jit(solution)/shard_map/ppermute | solution.py:255
  17.9 31.0 %collective-permute-start.1 = (f32[1,256]{1,0:T(1,128)S(1)}, f32[1,256]{1,0:T(1,128)S(1)}, u32[]{:S(2)}, u32[]{:S(2)}) collective-permute-start(f32[1,256]{1,0:T(1,128)S(1)} %bitcast.14), channel_id=1, source_target_pairs={{0,48},{48,0},{1,49},{49,1},{2,50},{50,2},{3,51},{51,3},{4,52},{52... | collective-permute-start | bytes 3080 | tf_op jit(solution)/shard_map/ppermute | solution.py:256
  51.0 4.6 %collective-permute-start.2 = (f32[8,272,128]{2,1,0:T(8,128)S(1)}, f32[8,272,128]{2,1,0:T(8,128)S(1)}, u32[]{:S(2)}, u32[]{:S(2)}) collective-permute-start(f32[8,272,128]{2,1,0:T(8,128)S(1)} %get-tuple-element.29), channel_id=1, source_target_pairs={{0,48},{48,0},{1,49},{49,1},{2,50},{50,2},{3,51},{51,3},{4,52},{52... | collective-permute-start | bytes 3342344 | tf_op jit(solution)/shard_map/ppermute | solution.py:275
  56.5 16.7 %all-to-all-start.1 = ((bf16[8,272,128]{2,1,0:T(8,128)(2,1)}), bf16[8,272,128]{2,1,0:T(8,128)(2,1)S(1)}, u32[]{:S(2)}, u32[]{:S(2)}) async-start(bf16[8,272,128]{2,1,0:T(8,128)(2,1)} %shard_map.80), calls=%async_computation.1 | async-start | bytes 1114112 | tf_op jit(solution)/shard_map/all_to_all | solution.py:51
  73.5 35.1 %all-to-all-start.2 = ((f16[8,64,640]{2,1,0:T(8,128)(2,1)}), f16[8,64,640]{2,1,0:T(8,128)(2,1)S(1)}, u32[]{:S(2)}, u32[]{:S(2)}) async-start(f16[8,64,640]{2,1,0:T(8,128)(2,1)} %convert_element_type.19), calls=%async_computation.2 | async-start | bytes 1310720 | tf_op jit(solution)/shard_map/all_to_all | solution.py:51
  108.6 4.4 %copy-start = (bf16[1,64,4096]{2,1,0:T(8,128)(2,1)S(1)}, bf16[1,64,4096]{2,1,0:T(8,128)(2,1)}, u32[]{:S(2)}) copy-start(bf16[1,64,4096]{2,1,0:T(8,128)(2,1)} %param.5) | copy-start | bytes 1572868
  108.6 4.4 %copy-start.2 = (f32[64,128]{1,0:T(8,128)S(1)}, f32[64,128]{1,0:T(8,128)}, u32[]{:S(2)}) copy-start(f32[64,128]{1,0:T(8,128)} %get-tuple-element.20.inv_ref) | copy-start | bytes 98308
  108.6 12.7 %all-to-all-start.3 = ((bf16[8,272,128]{2,1,0:T(8,128)(2,1)}), bf16[8,272,128]{2,1,0:T(8,128)(2,1)S(1)}, u32[]{:S(2)}, u32[]{:S(2)}) async-start(bf16[8,272,128]{2,1,0:T(8,128)(2,1)} %shard_map.83), calls=%async_computation.3 | async-start | bytes 1114112 | tf_op jit(solution)/shard_map/all_to_all | solution.py:51
